TPU v7x, 32 devices: a whole 2x2x4 slice. The times are simulated.
32 devices in a mesh: dp: 8 (over z, x), mp: 4 (over y, core).
Axes of the slice: x: 2, y: 2, z: 4, core: 2. Of those that a mesh axis runs over, the one named last changes fastest.
Arguments:
- features: bfloat16 [1024, 1536], P('dp', 'mp'), may hold values from -240 to 240
- proj_weight: bfloat16 [1536, 1152], P('mp'), may hold values from -0.15625 to 0.15625
- texts: bfloat16 [1024, 1152], P(('dp', 'mp')), may hold values from -6 to 6
Outputs:
- grad_features: bfloat16 [1024, 1536], P('dp', 'mp')
- grad_weight: float32 [1536, 1152], P('mp')
All inputs are finite; a program needn't handle non-finite values.
Results may differ from a plain program's by a relative error of at most 0.011.
Values may be sent and summed in bfloat16 or wider, within the bound.
No kernel may reach another device: no remote copies, remote signals or barrier semaphores. Data moves between devices by JAX's collectives and lax.ppermute only.
A program may use at most 64 MiB of HBM per device.

v0:
```python
import functools

import jax
import jax.numpy as jnp
from jax import lax
from jax.experimental import pallas as pl
from jax.experimental.pallas import tpu as pltpu
from jax.sharding import PartitionSpec as P

logit_scale = 100.0
logit_bias = -10.0
epsilon = 1e-06
LANES = 128
GATHER_BYTES = 8 << 20
VMEM_BYTES = 40 << 20
VMEM_ALL_BYTES = 62 << 20


def unit_rows(values):
    return values * lax.rsqrt(jnp.sum(values * values, axis=1, keepdims=True) + epsilon)


def add_texts(unit_img_b, image_ids, piece, piece_ids):
    unit_txt_b = unit_rows(piece.astype(jnp.float32)).astype(jnp.bfloat16)
    logits = (
        logit_scale * jnp.dot(unit_img_b, unit_txt_b.T, preferred_element_type=jnp.float32)
        + logit_bias
    )
    labels = jnp.where(image_ids[:, None] == piece_ids[None, :], 1.0, -1.0).astype(jnp.float32)
    slopes = (-labels * jax.nn.sigmoid(-labels * logits)).astype(jnp.bfloat16)
    return logit_scale * jnp.dot(slopes, unit_txt_b, preferred_element_type=jnp.float32)


def shards_summed(features, proj_weight, texts):
    local_rows = features.shape[0]
    width_local = features.shape[1]
    mp_count = lax.axis_size("mp")
    full_width = width_local * mp_count
    mp_index = lax.axis_index("mp")
    dp_index = lax.axis_index("dp")
    text_rows = texts.shape[0]
    inputs = features.astype(jnp.float32)
    mean_in = lax.psum(jnp.sum(inputs, axis=1, keepdims=True), "mp") / full_width
    centred = inputs - mean_in
    normed_b = centred.astype(jnp.bfloat16)
    partial_proj = jnp.dot(normed_b, proj_weight, preferred_element_type=jnp.float32)
    project = lax.psum(partial_proj, "mp")
    inv_norm = lax.rsqrt(jnp.sum(project * project, axis=1, keepdims=True) + epsilon)
    unit_img = project * inv_norm
    unit_img_b = unit_img.astype(jnp.bfloat16)
    image_ids = dp_index * local_rows + jnp.arange(local_rows, dtype=jnp.int32)
    piece = lax.all_gather(texts, "dp", axis=0, tiled=True)
    positions = jnp.arange(piece.shape[0], dtype=jnp.int32)
    shard_of = positions // text_rows
    piece_ids = (shard_of * mp_count + mp_index) * text_rows + positions % text_rows
    grad_unit = add_texts(unit_img_b, image_ids, piece, piece_ids)
    grad_unit = lax.psum(grad_unit, "mp")
    grad_proj = inv_norm * (
        grad_unit - unit_img * jnp.sum(unit_img * grad_unit, axis=1, keepdims=True)
    )
    grad_proj_b = grad_proj.astype(jnp.bfloat16)
    weight_part = jnp.dot(normed_b.T, grad_proj_b, preferred_element_type=jnp.float32)
    grad_weight = lax.psum(weight_part, "dp")
    grad_normed = jnp.dot(grad_proj_b, proj_weight.T, preferred_element_type=jnp.float32)
    grad_total = lax.psum(jnp.sum(grad_normed, axis=1, keepdims=True), "mp")
    grad_in = grad_normed - grad_total / full_width
    return (grad_in.astype(jnp.bfloat16), grad_weight)


def split_terms(value, count):
    terms = []
    for _ in range(count):
        term = value.astype(jnp.bfloat16).astype(jnp.float32)
        terms.append(term)
        value = value - term
    return terms


def kernel_call(body, outs, scratch=(), flops=0, vmem=VMEM_BYTES, **names):
    return pl.pallas_call(
        body,
        out_shape=outs,
        scratch_shapes=scratch,
        compiler_params=pltpu.CompilerParams(vmem_limit_bytes=vmem),
        cost_estimate=pl.CostEstimate(flops=flops, bytes_accessed=1 << 20, transcendentals=0),
        **names,
    )


def store_sums(extra_ref, column_sum, sum_row):
    extra_ref[...] = jnp.zeros_like(extra_ref)
    at = 0
    for term in split_terms(column_sum, 2):
        for i in range(column_sum.shape[1] // LANES):
            extra_ref[at : at + 1, :] = term[:, i * LANES : (i + 1) * LANES]
            at += 1
    for term in split_terms(sum_row, 3):
        extra_ref[at : at + 1, :] = term
        at += 1
    return extra_ref[...].astype(jnp.bfloat16)


def load_sums(extra, embed):
    chunks = embed // LANES
    extra = extra.astype(jnp.float32)
    column_sum = jnp.concatenate(
        [extra[i : i + 1] + extra[chunks + i : chunks + i + 1] for i in range(chunks)], axis=1
    )
    at = 2 * chunks
    return column_sum, extra[at : at + 1] + extra[at + 1 : at + 2] + extra[at + 2 : at + 3]


def pick_rows(sum_row, rows, group):
    row = lax.broadcasted_iota(jnp.int32, (rows, LANES), 0)
    lane = lax.broadcasted_iota(jnp.int32, (rows, LANES), 1)
    return jnp.sum(jnp.where(lane == row + group * rows, sum_row, 0.0), axis=1, keepdims=True)


def project_body(
    rows, mp_count, place_ref, features_hbm, weight_hbm, texts_hbm,
    keep_ref, send_ref, column_sum_ref, sum_row_ref, unit_txt_ref,
    extra_ref, features_ref, weight_ref, texts_ref, arrived,
):
    copies = [
        pltpu.make_async_copy(texts_hbm, texts_ref, arrived.at[0]),
        pltpu.make_async_copy(features_hbm, features_ref, arrived.at[1]),
        pltpu.make_async_copy(weight_hbm, weight_ref, arrived.at[2]),
    ]
    for copy in copies:
        copy.start()
    copies[0].wait()
    unit_txt_ref[...] = unit_rows(texts_ref[...].astype(jnp.float32)).astype(jnp.bfloat16)
    copies[1].wait()
    embed = weight_ref.shape[1]
    local_rows, width = features_ref.shape
    values = features_ref[...].astype(jnp.float32)
    row_sum = jnp.sum(values, axis=1, keepdims=True)
    row = lax.broadcasted_iota(jnp.int32, (local_rows, LANES), 0)
    lane = lax.broadcasted_iota(jnp.int32, (local_rows, LANES), 1)
    sum_row = jnp.sum(jnp.where(row == lane, row_sum, 0.0), axis=0, keepdims=True)
    ordered = []
    for flip in list(range(0, mp_count, 2)) + list(range(1, mp_count, 2)):
        start = pl.multiple_of(((place_ref[0] ^ flip) & (mp_count - 1)) * rows, rows)
        block = features_ref[pl.ds(start, rows), :].astype(jnp.float32)
        ordered.append(block - jnp.sum(block, axis=1, keepdims=True) / width)
    centred = jnp.concatenate(ordered, axis=0).astype(jnp.bfloat16)
    copies[2].wait()
    column_sum = jnp.sum(weight_ref[...].astype(jnp.float32), axis=0, keepdims=True)
    product = jnp.dot(centred, weight_ref[...], preferred_element_type=jnp.float32)
    half = local_rows // 2
    keep_ref[...] = product[:half]
    send_ref[:, :embed] = product[half:].astype(jnp.bfloat16)
    extra = store_sums(extra_ref, column_sum, sum_row)
    for i in range(half // rows):
        send_ref[i * rows : (i + 1) * rows, embed:] = extra
    column_sum_ref[...] = column_sum
    sum_row_ref[...] = sum_row


def chip_body(
    width, mp_count, place_ref, keep_ref, received_ref, column_sum_ref, sum_row_ref,
    own_ref, send_ref, chip_column_ref, chip_row_ref, extra_ref,
):
    rows = own_ref.shape[0]
    embed = own_ref.shape[1]
    columns = [column_sum_ref[...], None]
    sum_rows = [sum_row_ref[...], None]
    columns[1], sum_rows[1] = load_sums(received_ref[:rows, embed:], embed)
    chip_column = columns[0] + columns[1]
    chip_row = sum_rows[0] + sum_rows[1]
    for i in range(2):
        group = (place_ref[0] ^ (2 * i)) & (mp_count - 1)
        mean = pick_rows(chip_row, rows, group) / (2 * width)
        here = slice(i * rows, (i + 1) * rows)
        total = keep_ref[here, :] + received_ref[here, :embed].astype(jnp.float32)
        for column, sum_row in zip(columns, sum_rows):
            total = total + (pick_rows(sum_row, rows, group) / width - mean) * column
        if i == 0:
            own_ref[...] = total
        else:
            send_ref[:, :embed] = total.astype(jnp.bfloat16)
    send_ref[:, embed:] = store_sums(extra_ref, chip_column, chip_row)
    chip_column_ref[...] = chip_column
    chip_row_ref[...] = chip_row


def unit_body(
    full_width, mp_count, place_ref, features_ref, own_ref, received_ref, column_sum_ref,
    sum_row_ref, unit_b_ref, unit_ref, inv_norm_ref, normed_ref, weight_sum_ref,
):
    rows, embed = own_ref.shape
    columns = [column_sum_ref[...], None]
    sum_rows = [sum_row_ref[...], None]
    columns[1], sum_rows[1] = load_sums(received_ref[:, embed:], embed)
    group = place_ref[0] & (mp_count - 1)
    full_row = sum_rows[0] + sum_rows[1]
    mean = pick_rows(full_row, rows, group) / full_width
    project = own_ref[...] + received_ref[:, :embed].astype(jnp.float32)
    for column, sum_row in zip(columns, sum_rows):
        part_mean = pick_rows(sum_row, rows, group) / (full_width // 2)
        project = project + (part_mean - mean) * column
    inv_norm = lax.rsqrt(jnp.sum(project * project, axis=1, keepdims=True) + epsilon)
    unit_img = project * inv_norm
    unit_ref[...] = unit_img
    unit_b_ref[...] = unit_img.astype(jnp.bfloat16)
    inv_norm_ref[...] = inv_norm
    mean = pick_rows(full_row, features_ref.shape[0], 0) / full_width
    normed_ref[...] = (features_ref[...].astype(jnp.float32) - mean).astype(jnp.bfloat16)
    weight_sum_ref[...] = columns[0] + columns[1]


def slopes_body(images_a_ref, images_b_ref, texts_a_ref, texts_b_ref, keep_ref, send_ref):
    half, embed = images_a_ref.shape
    rows = half // 2
    unit_img_b = jnp.concatenate([images_a_ref[...], images_b_ref[...]], axis=0)
    unit_txt_b = jnp.concatenate([texts_a_ref[...], texts_b_ref[...]], axis=0)
    logits = (
        logit_scale
        * lax.dot_general(
            unit_img_b,
            unit_txt_b,
            (((1,), (1,)), ((), ())),
            preferred_element_type=jnp.float32,
        )
        + logit_bias
    )
    text = lax.broadcasted_iota(jnp.int32, logits.shape, 1)
    image = lax.broadcasted_iota(jnp.int32, logits.shape, 0)
    labels = jnp.where((text == image) & (image < rows), 1.0, -1.0)
    slopes = (-labels / (1.0 + jnp.exp(labels * logits))).astype(jnp.bfloat16)
    grad_unit = logit_scale * jnp.dot(slopes, unit_txt_b, preferred_element_type=jnp.float32)
    keep_ref[...] = grad_unit[:half]
    send_ref[...] = grad_unit[half:].astype(jnp.bfloat16)


def chip_grad_body(keep_ref, received_ref, own_ref, send_ref):
    rows = own_ref.shape[0]
    own_ref[...] = keep_ref[:rows, :] + received_ref[:rows, :].astype(jnp.float32)
    total = keep_ref[rows:, :] + received_ref[rows:, :].astype(jnp.float32)
    send_ref[...] = total.astype(jnp.bfloat16)


def grad_body(unit_ref, inv_norm_ref, own_ref, received_ref, out_ref):
    grad_unit = own_ref[...] + received_ref[...].astype(jnp.float32)
    unit_img = unit_ref[...]
    grad_proj = inv_norm_ref[...] * (
        grad_unit - unit_img * jnp.sum(unit_img * grad_unit, axis=1, keepdims=True)
    )
    out_ref[...] = grad_proj.astype(jnp.bfloat16)


def weight_body(rows, mp_count, line, normed_order, flip, place_ref, normed_ref, own_ref, other_ref,
                *refs):
    (*previous, out_ref) = refs
    blocks = []
    for i in range(2):
        group = (place_ref[0] ^ flip ^ i) & (mp_count - 1)
        for line_flip in line:
            start = (normed_order.index(line_flip) * mp_count + group) * rows
            blocks.append(normed_ref[pl.ds(pl.multiple_of(start, rows), rows), :])
    total = lax.dot_general(
        jnp.concatenate(blocks, axis=0),
        jnp.concatenate([own_ref[...], other_ref[...]], axis=0),
        (((0,), (0,)), ((), ())),
        preferred_element_type=jnp.float32,
    )
    for ref in previous:
        total = total + ref[...]
    out_ref[...] = total


def features_body(full_width, rows, mp_count, place_ref, weight_ref, weight_sum_ref, *refs):
    (*parts, out_ref, group_ref) = refs
    for flip, part in enumerate(parts):
        start = pl.multiple_of(((place_ref[0] ^ flip) & (mp_count - 1)) * rows, rows)
        group_ref[pl.ds(start, rows), :] = part[:rows, :]
    group = group_ref[...]
    grad_normed = lax.dot_general(
        group, weight_ref[...], (((1,), (1,)), ((), ())), preferred_element_type=jnp.float32
    )
    grad_total = jnp.sum(group.astype(jnp.float32) * weight_sum_ref[...], axis=1, keepdims=True)
    out_ref[...] = (grad_normed - grad_total / full_width).astype(jnp.bfloat16)


def shards_gathered(features, proj_weight, texts):
    axes = ("dp", "mp")
    dp_count, mp_count = lax.axis_size("dp"), lax.axis_size("mp")
    count = dp_count * mp_count
    plane_count = 2 * mp_count
    local_rows, width = features.shape
    embed = proj_weight.shape[1]
    rows = texts.shape[0]
    half = local_rows // 2
    full_width = width * mp_count
    place = (lax.axis_index("dp") * mp_count + lax.axis_index("mp")).astype(jnp.int32).reshape(1)
    core, across, column = 1, 2, mp_count
    line = list(range(count - plane_count, 0, -plane_count))

    def swap(value, flip):
        return lax.ppermute(value, axes, [(i, i ^ flip) for i in range(count)])

    def struct(dims, kind=jnp.bfloat16):
        return jax.ShapeDtypeStruct(dims, kind)

    def along_line(value):
        return jnp.concatenate([value] + [swap(value, flip) for flip in line], axis=0)

    smem = pl.BlockSpec(memory_space=pltpu.SMEM)
    vmem = pl.BlockSpec(memory_space=pltpu.VMEM)
    sums = [struct((1, embed), jnp.float32), struct((1, LANES), jnp.float32)]
    extra = pltpu.VMEM((rows, LANES), jnp.float32)

    hbm = pl.BlockSpec(memory_space=pltpu.HBM)
    keep, send, column_sum, sum_row, unit_txt_b = kernel_call(
        functools.partial(project_body, rows, mp_count),
        [struct((half, embed), jnp.float32), struct((half, embed + LANES))]
        + sums
        + [struct(texts.shape)],
        scratch=[
            extra,
            pltpu.VMEM(features.shape, features.dtype),
            pltpu.VMEM(proj_weight.shape, proj_weight.dtype),
            pltpu.VMEM(texts.shape, texts.dtype),
            pltpu.SemaphoreType.DMA((3,)),
        ],
        in_specs=[smem, hbm, hbm, hbm],
        flops=2 * local_rows * width * embed,
        vmem=VMEM_ALL_BYTES,
        name="project",
    )(place, features, proj_weight, texts)

    texts_a = along_line(unit_txt_b)
    texts_b = swap(texts_a, column)

    own, send, column_sum, sum_row = kernel_call(
        functools.partial(chip_body, width, mp_count),
        [struct((rows, embed), jnp.float32), struct((rows, embed + LANES))] + sums,
        scratch=[extra],
        in_specs=[smem] + [vmem] * 4,
        name="chip_project",
    )(place, keep, swap(send, core), column_sum, sum_row)
    unit_img_b, unit_img, inv_norm, normed_b, weight_sum = kernel_call(
        functools.partial(unit_body, full_width, mp_count),
        [
            struct((rows, embed)),
            struct((rows, embed), jnp.float32),
            struct((rows, 1), jnp.float32),
            struct((local_rows, width)),
            struct((1, embed), jnp.float32),
        ],
        in_specs=[smem] + [vmem] * 5,
        name="unit_images",
    )(place, features, own, swap(send, across), column_sum, sum_row)

    images_a = jnp.concatenate([unit_img_b, swap(unit_img_b, across)], axis=0)
    images_a, texts_a, normed_b = lax.optimization_barrier((images_a, texts_a, normed_b))
    images_b = swap(images_a, core)
    normed_line, normed_order = normed_b, [0]
    far, near = line[len(line) // 2], line[-1]
    normed_line = jnp.concatenate([normed_line, swap(normed_line, far)], axis=0)

    keep, send = kernel_call(
        slopes_body,
        [struct((half, embed), jnp.float32), struct((half, embed))],
        flops=4 * local_rows * local_rows * 2 * embed,
        name="slopes",
    )(images_a, images_b, texts_a, texts_b)
    send, normed_line = lax.optimization_barrier((send, normed_line))
    normed_line = jnp.concatenate([normed_line, swap(normed_line, near)], axis=0)
    normed_order = [0, far, near, far ^ near]
    own, send = kernel_call(
        chip_grad_body,
        [struct((rows, embed), jnp.float32), struct((rows, embed))],
        name="chip_grad",
    )(keep, swap(send, core))
    received = swap(send, across)
    received, normed_line = lax.optimization_barrier((received, normed_line))
    normed_other = swap(normed_line, column)
    grad_rows = kernel_call(grad_body, struct((rows, embed)), name="grad_project")(
        unit_img, inv_norm, own, received
    )

    grad_line = along_line(grad_rows)
    grad_line, normed_other = lax.optimization_barrier((grad_line, normed_other))
    plane = [0, across, column, column | across]
    grads = [grad_line] + [swap(grad_line, flip) for flip in plane[1:]]
    others = [swap(value, core) for value in grads[:2]]
    group = [grads[0], others[0], grads[1], others[1]]
    grad_features = kernel_call(
        functools.partial(features_body, full_width, rows, mp_count),
        struct(features.shape),
        scratch=[pltpu.VMEM((local_rows, embed), jnp.bfloat16)],
        in_specs=[smem] + [vmem] * (2 + mp_count),
        flops=2 * local_rows * width * embed,
        name="grad_features",
    )(place, proj_weight, weight_sum, *group)

    def add_product(index, previous):
        return kernel_call(
            functools.partial(
                weight_body, rows, mp_count, [0] + line, normed_order, plane[index]
            ),
            struct(proj_weight.shape, jnp.float32),
            in_specs=[smem] + [vmem] * (3 + len(previous)),
            flops=4 * width * embed * local_rows,
            name="weight",
        )(
            place,
            normed_other if plane[index] & column else normed_line,
            grads[index],
            others[index],
            *previous,
        )

    grad_weight = add_product(0, [])
    grads[2], grad_weight = lax.optimization_barrier((grads[2], grad_weight))
    others.append(swap(grads[2], core))
    grad_weight = add_product(1, [grad_weight])
    grads[3], grad_weight, grad_features = lax.optimization_barrier(
        (grads[3], grad_weight, grad_features)
    )
    others.append(swap(grads[3], core))
    grad_weight = add_product(2, [grad_weight])
    grad_weight = add_product(3, [grad_weight])
    return grad_features, grad_weight


def shards(features, proj_weight, texts):
    dp_count, mp_count = lax.axis_size("dp"), lax.axis_size("mp")
    count = dp_count * mp_count
    rows = texts.shape[0]
    embed = texts.shape[1]
    fits = (
        count * rows * (embed + LANES) * 2 <= GATHER_BYTES
        and count & (count - 1) == 0
        and mp_count == 4
        and count == 8 * mp_count
        and features.shape[0] == LANES == mp_count * rows
        and embed % LANES == 0
        and 2 * (embed // LANES) + 3 <= rows
        and rows % 16 == 0
    )
    plan = shards_gathered if fits else shards_summed
    return plan(features, proj_weight, texts)


def solution(mesh):
    return jax.shard_map(
        shards,
        mesh=mesh,
        in_specs=(P("dp", "mp"), P("mp", None), P(("dp", "mp"), None)),
        out_specs=(P("dp", "mp"), P("mp", None)),
        check_vma=False,
    )
```

profile of v0, /device:TPU:0, one launch (start us, length us, event | category | flops | bytes accessed | tf_op | source)
XLA Modules:
  0.0 72.0 jit_solution(8985250461950268168)
XLA Ops:
  0.6 2.4 %project.1 = (f32[64,1152]{1,0:T(8,128)}, bf16[64,1280]{1,0:T(8,128)(2,1)}, f32[1,1152]{1,0:T(1,128)}, f32[1,128]{1,0:T(1,128)}, bf16[32,1152]{1,0:T(8,128)(2,1)}) custom-call(s32[1]{0:T(128)} %bitcast.place_ref, bf16[128,384]{1,0:T(8,128)(2,1)} %features_ref.1, bf16[384,1152]{1,0:T(8,128)(2,1)} %weight_ref.1, bf16[32,1152]{1,0:T(8,128)(2,1)} %texts_hbm.1), custom_call_target="tpu_custom_call" | custom-call | flops 113246208 | bytes 1048576 | tf_op jit(solution)/shard_map/project/pallas_call | solution.py:314
  3.1 3.1 %collective-permute-start.5 = (bf16[32,1152]{1,0:T(8,128)(2,1)}, bf16[32,1152]{1,0:T(8,128)(2,1)S(1)}, u32[]{:S(2)}, u32[]{:S(2)}) collective-permute-start(bf16[32,1152]{1,0:T(8,128)(2,1)} %get-tuple-element.45), channel_id=1, source_target_pairs={{0,8},{1,9},{2,10},{3,11},{4,12},{5,13},{6,14},{7,15},{8,0},{9,1},... | collective-permute-start | bytes 221192 | tf_op jit(solution)/shard_map/ppermute | solution.py:300
  6.2 2.6 %collective-permute-start.4 = (bf16[32,1152]{1,0:T(8,128)(2,1)}, bf16[32,1152]{1,0:T(8,128)(2,1)S(1)}, u32[]{:S(2)}, u32[]{:S(2)}) collective-permute-start(bf16[32,1152]{1,0:T(8,128)(2,1)} %get-tuple-element.45), channel_id=1, source_target_pairs={{0,16},{1,17},{2,18},{3,19},{4,20},{5,21},{6,22},{7,23},{8,24},{9,... | collective-permute-start | bytes 221192 | tf_op jit(solution)/shard_map/ppermute | solution.py:300
  9.7 5.5 %collective-permute-done.3 = bf16[32,1152]{1,0:T(8,128)(2,1)S(1)} collective-permute-done((bf16[32,1152]{1,0:T(8,128)(2,1)}, bf16[32,1152]{1,0:T(8,128)(2,1)S(1)}, u32[]{:S(2)}, u32[]{:S(2)}) %collective-permute-start.3) | collective-permute-done | bytes 73760 | tf_op jit(solution)/shard_map/ppermute | solution.py:300
  17.6 1.6 %collective-permute-start.1 = (bf16[32,1280]{1,0:T(8,128)(2,1)S(1)}, bf16[32,1280]{1,0:T(8,128)(2,1)S(1)}, u32[]{:S(2)}, u32[]{:S(2)}) collective-permute-start(bf16[32,1280]{1,0:T(8,128)(2,1)S(1)} %get-tuple-element.39), channel_id=1, source_target_pairs={{0,2},{1,3},{2,0},{3,1},{4,6},{5,7},{6,4},{7,5},{8,10},{9,11},{10,... | collective-permute-start | bytes 245768 | tf_op jit(solution)/shard_map/ppermute | solution.py:300
  19.3 3.2 %collective-permute-done.1.received_ref = bf16[32,1280]{1,0:T(8,128)(2,1)S(1)} collective-permute-done((bf16[32,1280]{1,0:T(8,128)(2,1)S(1)}, bf16[32,1280]{1,0:T(8,128)(2,1)S(1)}, u32[]{:S(2)}, u32[]{:S(2)}) %collective-permute-start.1) | collective-permute-done | bytes 81952 | tf_op jit(solution)/shard_map/ppermute | solution.py:300
  22.7 1.6 %collective-permute-start.2 = (bf16[32,1152]{1,0:T(8,128)(2,1)S(1)}, bf16[32,1152]{1,0:T(8,128)(2,1)S(1)}, u32[]{:S(2)}, u32[]{:S(2)}) collective-permute-start(bf16[32,1152]{1,0:T(8,128)(2,1)S(1)} %get-tuple-element.44), channel_id=1, source_target_pairs={{0,2},{1,3},{2,0},{3,1},{4,6},{5,7},{6,4},{7,5},{8,10},{9,11},{10,... | collective-permute-start | bytes 221192 | tf_op jit(solution)/shard_map/ppermute | solution.py:300
  24.3 1.6 %collective-permute-start.7 = (bf16[128,1152]{1,0:T(8,128)(2,1)S(1)}, bf16[128,1152]{1,0:T(8,128)(2,1)S(1)}, u32[]{:S(2)}, u32[]{:S(2)}) collective-permute-start(bf16[128,1152]{1,0:T(8,128)(2,1)S(1)} %constant_dynamic-update-slice_fusion.texts_a_ref), channel_id=1, source_target_pairs={{0,4},{1,5},{2,6},{3,7},{4,0},{5,1},{6,2},{7,3},{8,12},{9,13},{10,... | collective-permute-start | bytes 884744 | tf_op jit(solution)/shard_map/ppermute | solution.py:300
  25.8 1.3 %collective-permute-done.2 = bf16[32,1152]{1,0:T(8,128)(2,1)S(1)} collective-permute-done((bf16[32,1152]{1,0:T(8,128)(2,1)S(1)}, bf16[32,1152]{1,0:T(8,128)(2,1)S(1)}, u32[]{:S(2)}, u32[]{:S(2)}) %collective-permute-start.2) | collective-permute-done | bytes 73760 | tf_op jit(solution)/shard_map/ppermute | solution.py:300
  27.1 1.9 %collective-permute-start.8 = (bf16[128,384]{1,0:T(8,128)(2,1)S(1)}, bf16[128,384]{1,0:T(8,128)(2,1)S(1)}, u32[]{:S(2)}, u32[]{:S(2)}) collective-permute-start(bf16[128,384]{1,0:T(8,128)(2,1)S(1)} %get-tuple-element.51), channel_id=1, source_target_pairs={{0,16},{1,17},{2,18},{3,19},{4,20},{5,21},{6,22},{7,23},{8,24},{9,... | collective-permute-start | bytes 294920 | tf_op jit(solution)/shard_map/ppermute | solution.py:300
  29.0 4.8 %collective-permute-done.8 = bf16[128,384]{1,0:T(8,128)(2,1)S(1)} collective-permute-done((bf16[128,384]{1,0:T(8,128)(2,1)S(1)}, bf16[128,384]{1,0:T(8,128)(2,1)S(1)}, u32[]{:S(2)}, u32[]{:S(2)}) %collective-permute-start.8) | collective-permute-done | bytes 98336 | tf_op jit(solution)/shard_map/ppermute | solution.py:300
  34.6 1.4 %collective-permute-done.9.received_ref = bf16[64,1152]{1,0:T(8,128)(2,1)S(1)} collective-permute-done((bf16[64,1152]{1,0:T(8,128)(2,1)S(1)}, bf16[64,1152]{1,0:T(8,128)(2,1)S(1)}, u32[]{:S(2)}, u32[]{:S(2)}) %collective-permute-start.9) | collective-permute-done | bytes 147488 | tf_op jit(solution)/shard_map/ppermute | solution.py:300
  36.0 1.6 %collective-permute-start.10 = (bf16[32,1152]{1,0:T(8,128)(2,1)S(1)}, bf16[32,1152]{1,0:T(8,128)(2,1)S(1)}, u32[]{:S(2)}, u32[]{:S(2)}) collective-permute-start(bf16[32,1152]{1,0:T(8,128)(2,1)S(1)} %get-tuple-element.54), channel_id=1, source_target_pairs={{0,2},{1,3},{2,0},{3,1},{4,6},{5,7},{6,4},{7,5},{8,10},{9,11},{10,... | collective-permute-start | bytes 221192 | tf_op jit(solution)/shard_map/ppermute | solution.py:300
  37.6 2.6 %collective-permute-done.11 = bf16[256,384]{1,0:T(8,128)(2,1)S(1)} collective-permute-done((bf16[256,384]{1,0:T(8,128)(2,1)S(1)}, bf16[256,384]{1,0:T(8,128)(2,1)S(1)}, u32[]{:S(2)}, u32[]{:S(2)}) %collective-permute-start.11) | collective-permute-done | bytes 196640 | tf_op jit(solution)/shard_map/ppermute | solution.py:300
  40.4 1.5 %collective-permute-start.15 = (bf16[512,384]{1,0:T(8,128)(2,1)S(1)}, bf16[512,384]{1,0:T(8,128)(2,1)S(1)}, u32[]{:S(2)}, u32[]{:S(2)}) collective-permute-start(bf16[512,384]{1,0:T(8,128)(2,1)S(1)} %pad_maximum_fusion.normed_ref), channel_id=1, source_target_pairs={{0,4},{1,5},{2,6},{3,7},{4,0},{5,1},{6,2},{7,3},{8,12},{9,13},{10,... | collective-permute-start | bytes 1179656 | tf_op jit(solution)/shard_map/ppermute | solution.py:300
  42.1 2.0 %collective-permute-start.14 = (bf16[32,1152]{1,0:T(8,128)(2,1)S(1)}, bf16[32,1152]{1,0:T(8,128)(2,1)S(1)}, u32[]{:S(2)}, u32[]{:S(2)}) collective-permute-start(bf16[32,1152]{1,0:T(8,128)(2,1)S(1)} %grad_project.1), channel_id=1, source_target_pairs={{0,8},{1,9},{2,10},{3,11},{4,12},{5,13},{6,14},{7,15},{8,0},{9,1},... | collective-permute-start | bytes 221192 | tf_op jit(solution)/shard_map/ppermute | solution.py:300
  44.8 1.7 %collective-permute-start.12 = (bf16[32,1152]{1,0:T(8,128)(2,1)S(1)}, bf16[32,1152]{1,0:T(8,128)(2,1)S(1)}, u32[]{:S(2)}, u32[]{:S(2)}) collective-permute-start(bf16[32,1152]{1,0:T(8,128)(2,1)S(1)} %grad_project.1), channel_id=1, source_target_pairs={{0,24},{1,25},{2,26},{3,27},{4,28},{5,29},{6,30},{7,31},{8,16},{9,... | collective-permute-start | bytes 221192 | tf_op jit(solution)/shard_map/ppermute | solution.py:300
  47.0 4.5 %collective-permute-done.13 = bf16[32,1152]{1,0:T(8,128)(2,1)S(1)} collective-permute-done((bf16[32,1152]{1,0:T(8,128)(2,1)S(1)}, bf16[32,1152]{1,0:T(8,128)(2,1)S(1)}, u32[]{:S(2)}, u32[]{:S(2)}) %collective-permute-start.13) | collective-permute-done | bytes 73760 | tf_op jit(solution)/shard_map/ppermute | solution.py:300
  51.5 1.6 %collective-permute-start.17 = (bf16[128,1152]{1,0:T(8,128)(2,1)S(1)}, bf16[128,1152]{1,0:T(8,128)(2,1)S(1)}, u32[]{:S(2)}, u32[]{:S(2)}) collective-permute-start(bf16[128,1152]{1,0:T(8,128)(2,1)S(1)} %pad_maximum_fusion.1.own_ref.refs_0_), channel_id=1, source_target_pairs={{0,2},{1,3},{2,0},{3,1},{4,6},{5,7},{6,4},{7,5},{8,10},{9,11},{10,... | collective-permute-start | bytes 884744 | tf_op jit(solution)/shard_map/ppermute | solution.py:300
  53.8 4.5 %collective-permute-done.17.own_ref.refs_2_ = bf16[128,1152]{1,0:T(8,128)(2,1)S(1)} collective-permute-done((bf16[128,1152]{1,0:T(8,128)(2,1)S(1)}, bf16[128,1152]{1,0:T(8,128)(2,1)S(1)}, u32[]{:S(2)}, u32[]{:S(2)}) %collective-permute-start.17) | collective-permute-done | bytes 294944 | tf_op jit(solution)/shard_map/ppermute | solution.py:300
  58.3 2.2 %collective-permute-start.16 = (bf16[128,1152]{1,0:T(8,128)(2,1)S(1)}, bf16[128,1152]{1,0:T(8,128)(2,1)S(1)}, u32[]{:S(2)}, u32[]{:S(2)}) collective-permute-start(bf16[128,1152]{1,0:T(8,128)(2,1)S(1)} %pad_maximum_fusion.1.own_ref.refs_0_), channel_id=1, source_target_pairs={{0,6},{1,7},{2,4},{3,5},{4,2},{5,3},{6,0},{7,1},{8,14},{9,15},{10,... | collective-permute-start | bytes 884744 | tf_op jit(solution)/shard_map/ppermute | solution.py:300
  61.0 1.6 %collective-permute-done.19.own_ref = bf16[128,1152]{1,0:T(8,128)(2,1)S(1)} collective-permute-done((bf16[128,1152]{1,0:T(8,128)(2,1)S(1)}, bf16[128,1152]{1,0:T(8,128)(2,1)S(1)}, u32[]{:S(2)}, u32[]{:S(2)}) %collective-permute-start.19) | collective-permute-done | bytes 294944 | tf_op jit(solution)/shard_map/ppermute | solution.py:300
  64.2 4.6 %collective-permute-done.16.own_ref = bf16[128,1152]{1,0:T(8,128)(2,1)S(1)} collective-permute-done((bf16[128,1152]{1,0:T(8,128)(2,1)S(1)}, bf16[128,1152]{1,0:T(8,128)(2,1)S(1)}, u32[]{:S(2)}, u32[]{:S(2)}) %collective-permute-start.16) | collective-permute-done | bytes 294944 | tf_op jit(solution)/shard_map/ppermute | solution.py:300
  70.3 1.7 %weight.7 = f32[384,1152]{1,0:T(8,128)} custom-call(s32[1]{0:T(128)} %bitcast.place_ref, bf16[512,384]{1,0:T(8,128)(2,1)S(1)} %collective-permute-done.15.normed_ref, bf16[128,1152]{1,0:T(8,128)(2,1)S(1)} %collective-permute-done.16.own_ref, bf16[128,1152]{1,0:T(8,128)(2,1)S(1)} %collective-permute-done.21.other_ref, f32[384,1152]{1,0:T(8,128)S(1)} %weight.6.refs_0_), custom_call_target="tpu_custom_call" | custom-call | flops 226492416 | bytes 1048576 | tf_op jit(solution)/shard_map/weight/pallas_call | solution.py:399
  (51 shorter events, 10.4 us)
Async XLA Ops:
  0.6 21.8 %copy-start.1 = (bf16[128,384]{1,0:T(8,128)(2,1)S(1)}, bf16[128,384]{1,0:T(8,128)(2,1)}, u32[]{:S(2)}) copy-start(bf16[128,384]{1,0:T(8,128)(2,1)} %features_ref.1) | copy-start | bytes 294916
  3.1 21.2 %collective-permute-start.5 = (bf16[32,1152]{1,0:T(8,128)(2,1)}, bf16[32,1152]{1,0:T(8,128)(2,1)S(1)}, u32[]{:S(2)}, u32[]{:S(2)}) collective-permute-start(bf16[32,1152]{1,0:T(8,128)(2,1)} %get-tuple-element.45), channel_id=1, source_target_pairs={{0,8},{1,9},{2,10},{3,11},{4,12},{5,13},{6,14},{7,15},{8,0},{9,1},... | collective-permute-start | bytes 221192 | tf_op jit(solution)/shard_map/ppermute | solution.py:300
  6.2 13.1 %collective-permute-start.4 = (bf16[32,1152]{1,0:T(8,128)(2,1)}, bf16[32,1152]{1,0:T(8,128)(2,1)S(1)}, u32[]{:S(2)}, u32[]{:S(2)}) collective-permute-start(bf16[32,1152]{1,0:T(8,128)(2,1)} %get-tuple-element.45), channel_id=1, source_target_pairs={{0,16},{1,17},{2,18},{3,19},{4,20},{5,21},{6,22},{7,23},{8,24},{9,... | collective-permute-start | bytes 221192 | tf_op jit(solution)/shard_map/ppermute | solution.py:300
  8.7 6.5 %collective-permute-start.3 = (bf16[32,1152]{1,0:T(8,128)(2,1)}, bf16[32,1152]{1,0:T(8,128)(2,1)S(1)}, u32[]{:S(2)}, u32[]{:S(2)}) collective-permute-start(bf16[32,1152]{1,0:T(8,128)(2,1)} %get-tuple-element.45), channel_id=1, source_target_pairs={{0,24},{1,25},{2,26},{3,27},{4,28},{5,29},{6,30},{7,31},{8,16},{9,... | collective-permute-start | bytes 221192 | tf_op jit(solution)/shard_map/ppermute | solution.py:300
  8.7 6.5 %collective-permute-start = (bf16[64,1280]{1,0:T(8,128)(2,1)}, bf16[64,1280]{1,0:T(8,128)(2,1)S(1)}, u32[]{:S(2)}, u32[]{:S(2)}) collective-permute-start(bf16[64,1280]{1,0:T(8,128)(2,1)} %get-tuple-element.35), channel_id=1, source_target_pairs={{0,1},{1,0},{2,3},{3,2},{4,5},{5,4},{6,7},{7,6},{8,9},{9,8},{10,11... | collective-permute-start | bytes 491528 | tf_op jit(solution)/shard_map/ppermute | solution.py:300
  17.6 4.8 %collective-permute-start.1 = (bf16[32,1280]{1,0:T(8,128)(2,1)S(1)}, bf16[32,1280]{1,0:T(8,128)(2,1)S(1)}, u32[]{:S(2)}, u32[]{:S(2)}) collective-permute-start(bf16[32,1280]{1,0:T(8,128)(2,1)S(1)} %get-tuple-element.39), channel_id=1, source_target_pairs={{0,2},{1,3},{2,0},{3,1},{4,6},{5,7},{6,4},{7,5},{8,10},{9,11},{10,... | collective-permute-start | bytes 245768 | tf_op jit(solution)/shard_map/ppermute | solution.py:300
  22.7 4.4 %collective-permute-start.2 = (bf16[32,1152]{1,0:T(8,128)(2,1)S(1)}, bf16[32,1152]{1,0:T(8,128)(2,1)S(1)}, u32[]{:S(2)}, u32[]{:S(2)}) collective-permute-start(bf16[32,1152]{1,0:T(8,128)(2,1)S(1)} %get-tuple-element.44), channel_id=1, source_target_pairs={{0,2},{1,3},{2,0},{3,1},{4,6},{5,7},{6,4},{7,5},{8,10},{9,11},{10,... | collective-permute-start | bytes 221192 | tf_op jit(solution)/shard_map/ppermute | solution.py:300
  24.3 9.5 %collective-permute-start.7 = (bf16[128,1152]{1,0:T(8,128)(2,1)S(1)}, bf16[128,1152]{1,0:T(8,128)(2,1)S(1)}, u32[]{:S(2)}, u32[]{:S(2)}) collective-permute-start(bf16[128,1152]{1,0:T(8,128)(2,1)S(1)} %constant_dynamic-update-slice_fusion.texts_a_ref), channel_id=1, source_target_pairs={{0,4},{1,5},{2,6},{3,7},{4,0},{5,1},{6,2},{7,3},{8,12},{9,13},{10,... | collective-permute-start | bytes 884744 | tf_op jit(solution)/shard_map/ppermute | solution.py:300
  27.1 6.6 %collective-permute-start.8 = (bf16[128,384]{1,0:T(8,128)(2,1)S(1)}, bf16[128,384]{1,0:T(8,128)(2,1)S(1)}, u32[]{:S(2)}, u32[]{:S(2)}) collective-permute-start(bf16[128,384]{1,0:T(8,128)(2,1)S(1)} %get-tuple-element.51), channel_id=1, source_target_pairs={{0,16},{1,17},{2,18},{3,19},{4,20},{5,21},{6,22},{7,23},{8,24},{9,... | collective-permute-start | bytes 294920 | tf_op jit(solution)/shard_map/ppermute | solution.py:300
  29.0 4.8 %collective-permute-start.6 = (bf16[64,1152]{1,0:T(8,128)(2,1)S(1)}, bf16[64,1152]{1,0:T(8,128)(2,1)S(1)}, u32[]{:S(2)}, u32[]{:S(2)}) collective-permute-start(bf16[64,1152]{1,0:T(8,128)(2,1)S(1)} %pad_maximum_fusion.3.images_a_ref), channel_id=1, source_target_pairs={{0,1},{1,0},{2,3},{3,2},{4,5},{5,4},{6,7},{7,6},{8,9},{9,8},{10,11... | collective-permute-start | bytes 442376 | tf_op jit(solution)/shard_map/ppermute | solution.py:300
  34.5 5.7 %collective-permute-start.11 = (bf16[256,384]{1,0:T(8,128)(2,1)S(1)}, bf16[256,384]{1,0:T(8,128)(2,1)S(1)}, u32[]{:S(2)}, u32[]{:S(2)}) collective-permute-start(bf16[256,384]{1,0:T(8,128)(2,1)S(1)} %pad_maximum_fusion.2), channel_id=1, source_target_pairs={{0,8},{1,9},{2,10},{3,11},{4,12},{5,13},{6,14},{7,15},{8,0},{9,1},... | collective-permute-start | bytes 589832 | tf_op jit(solution)/shard_map/ppermute | solution.py:300
  34.6 1.4 %collective-permute-start.9 = (bf16[64,1152]{1,0:T(8,128)(2,1)S(1)}, bf16[64,1152]{1,0:T(8,128)(2,1)S(1)}, u32[]{:S(2)}, u32[]{:S(2)}) collective-permute-start(bf16[64,1152]{1,0:T(8,128)(2,1)S(1)} %get-tuple-element.52), channel_id=1, source_target_pairs={{0,1},{1,0},{2,3},{3,2},{4,5},{5,4},{6,7},{7,6},{8,9},{9,8},{10,11... | collective-permute-start | bytes 442376 | tf_op jit(solution)/shard_map/ppermute | solution.py:300
  36.0 4.4 %collective-permute-start.10 = (bf16[32,1152]{1,0:T(8,128)(2,1)S(1)}, bf16[32,1152]{1,0:T(8,128)(2,1)S(1)}, u32[]{:S(2)}, u32[]{:S(2)}) collective-permute-start(bf16[32,1152]{1,0:T(8,128)(2,1)S(1)} %get-tuple-element.54), channel_id=1, source_target_pairs={{0,2},{1,3},{2,0},{3,1},{4,6},{5,7},{6,4},{7,5},{8,10},{9,11},{10,... | collective-permute-start | bytes 221192 | tf_op jit(solution)/shard_map/ppermute | solution.py:300
  40.4 11.0 %collective-permute-start.15 = (bf16[512,384]{1,0:T(8,128)(2,1)S(1)}, bf16[512,384]{1,0:T(8,128)(2,1)S(1)}, u32[]{:S(2)}, u32[]{:S(2)}) collective-permute-start(bf16[512,384]{1,0:T(8,128)(2,1)S(1)} %pad_maximum_fusion.normed_ref), channel_id=1, source_target_pairs={{0,4},{1,5},{2,6},{3,7},{4,0},{5,1},{6,2},{7,3},{8,12},{9,13},{10,... | collective-permute-start | bytes 1179656 | tf_op jit(solution)/shard_map/ppermute | solution.py:300
  42.1 4.9 %collective-permute-start.14 = (bf16[32,1152]{1,0:T(8,128)(2,1)S(1)}, bf16[32,1152]{1,0:T(8,128)(2,1)S(1)}, u32[]{:S(2)}, u32[]{:S(2)}) collective-permute-start(bf16[32,1152]{1,0:T(8,128)(2,1)S(1)} %grad_project.1), channel_id=1, source_target_pairs={{0,8},{1,9},{2,10},{3,11},{4,12},{5,13},{6,14},{7,15},{8,0},{9,1},... | collective-permute-start | bytes 221192 | tf_op jit(solution)/shard_map/ppermute | solution.py:300
  44.1 7.3 %collective-permute-start.13 = (bf16[32,1152]{1,0:T(8,128)(2,1)S(1)}, bf16[32,1152]{1,0:T(8,128)(2,1)S(1)}, u32[]{:S(2)}, u32[]{:S(2)}) collective-permute-start(bf16[32,1152]{1,0:T(8,128)(2,1)S(1)} %grad_project.1), channel_id=1, source_target_pairs={{0,16},{1,17},{2,18},{3,19},{4,20},{5,21},{6,22},{7,23},{8,24},{9,... | collective-permute-start | bytes 221192 | tf_op jit(solution)/shard_map/ppermute | solution.py:300
  44.8 6.6 %collective-permute-start.12 = (bf16[32,1152]{1,0:T(8,128)(2,1)S(1)}, bf16[32,1152]{1,0:T(8,128)(2,1)S(1)}, u32[]{:S(2)}, u32[]{:S(2)}) collective-permute-start(bf16[32,1152]{1,0:T(8,128)(2,1)S(1)} %grad_project.1), channel_id=1, source_target_pairs={{0,24},{1,25},{2,26},{3,27},{4,28},{5,29},{6,30},{7,31},{8,16},{9,... | collective-permute-start | bytes 221192 | tf_op jit(solution)/shard_map/ppermute | solution.py:300
  51.5 6.8 %collective-permute-start.17 = (bf16[128,1152]{1,0:T(8,128)(2,1)S(1)}, bf16[128,1152]{1,0:T(8,128)(2,1)S(1)}, u32[]{:S(2)}, u32[]{:S(2)}) collective-permute-start(bf16[128,1152]{1,0:T(8,128)(2,1)S(1)} %pad_maximum_fusion.1.own_ref.refs_0_), channel_id=1, source_target_pairs={{0,2},{1,3},{2,0},{3,1},{4,6},{5,7},{6,4},{7,5},{8,10},{9,11},{10,... | collective-permute-start | bytes 884744 | tf_op jit(solution)/shard_map/ppermute | solution.py:300
  53.1 7.4 %collective-permute-start.20 = (bf16[128,1152]{1,0:T(8,128)(2,1)S(1)}, bf16[128,1152]{1,0:T(8,128)(2,1)S(1)}, u32[]{:S(2)}, u32[]{:S(2)}) collective-permute-start(bf16[128,1152]{1,0:T(8,128)(2,1)S(1)} %pad_maximum_fusion.1.own_ref.refs_0_), channel_id=1, source_target_pairs={{0,1},{1,0},{2,3},{3,2},{4,5},{5,4},{6,7},{7,6},{8,9},{9,8},{10,11... | collective-permute-start | bytes 884744 | tf_op jit(solution)/shard_map/ppermute | solution.py:300
  53.1 9.5 %collective-permute-start.19 = (bf16[128,1152]{1,0:T(8,128)(2,1)S(1)}, bf16[128,1152]{1,0:T(8,128)(2,1)S(1)}, u32[]{:S(2)}, u32[]{:S(2)}) collective-permute-start(bf16[128,1152]{1,0:T(8,128)(2,1)S(1)} %pad_maximum_fusion.1.own_ref.refs_0_), channel_id=1, source_target_pairs={{0,4},{1,5},{2,6},{3,7},{4,0},{5,1},{6,2},{7,3},{8,12},{9,13},{10,... | collective-permute-start | bytes 884744 | tf_op jit(solution)/shard_map/ppermute | solution.py:300
  58.3 4.3 %collective-permute-start.18 = (bf16[128,1152]{1,0:T(8,128)(2,1)S(1)}, bf16[128,1152]{1,0:T(8,128)(2,1)S(1)}, u32[]{:S(2)}, u32[]{:S(2)}) collective-permute-start(bf16[128,1152]{1,0:T(8,128)(2,1)S(1)} %collective-permute-done.17.own_ref.refs_2_), channel_id=1, source_target_pairs={{0,1},{1,0},{2,3},{3,2},{4,5},{5,4},{6,7},{7,6},{8,9},{9,8},{10,11... | collective-permute-start | bytes 884744 | tf_op jit(solution)/shard_map/ppermute | solution.py:300
  58.3 10.5 %collective-permute-start.16 = (bf16[128,1152]{1,0:T(8,128)(2,1)S(1)}, bf16[128,1152]{1,0:T(8,128)(2,1)S(1)}, u32[]{:S(2)}, u32[]{:S(2)}) collective-permute-start(bf16[128,1152]{1,0:T(8,128)(2,1)S(1)} %pad_maximum_fusion.1.own_ref.refs_0_), channel_id=1, source_target_pairs={{0,6},{1,7},{2,4},{3,5},{4,2},{5,3},{6,0},{7,1},{8,14},{9,15},{10,... | collective-permute-start | bytes 884744 | tf_op jit(solution)/shard_map/ppermute | solution.py:300
  62.6 6.2 %collective-permute-start.22 = (bf16[128,1152]{1,0:T(8,128)(2,1)S(1)}, bf16[128,1152]{1,0:T(8,128)(2,1)S(1)}, u32[]{:S(2)}, u32[]{:S(2)}) collective-permute-start(bf16[128,1152]{1,0:T(8,128)(2,1)S(1)} %collective-permute-done.19.own_ref), channel_id=1, source_target_pairs={{0,1},{1,0},{2,3},{3,2},{4,5},{5,4},{6,7},{7,6},{8,9},{9,8},{10,11... | collective-permute-start | bytes 884744 | tf_op jit(solution)/shard_map/ppermute | solution.py:300
  68.7 1.6 %collective-permute-start.21 = (bf16[128,1152]{1,0:T(8,128)(2,1)S(1)}, bf16[128,1152]{1,0:T(8,128)(2,1)S(1)}, u32[]{:S(2)}, u32[]{:S(2)}) collective-permute-start(bf16[128,1152]{1,0:T(8,128)(2,1)S(1)} %collective-permute-done.16.own_ref), channel_id=1, source_target_pairs={{0,1},{1,0},{2,3},{3,2},{4,5},{5,4},{6,7},{7,6},{8,9},{9,8},{10,11... | collective-permute-start | bytes 884744 | tf_op jit(solution)/shard_map/ppermute | solution.py:300
  (4 other events, 22.8 us)
where the time goes:
time: 72.3 us; the launch traced here: 72 us
  waiting for transfers between devices  35.6 us (49%)
  starting transfers between devices  24.5 us (34%)
  Pallas kernels  7.81 us (11%)
  local copies, waits for them, and re-layouts  3.25 us (4%)
  between operations  0.79 us (1%)
    ppermute x23, waiting for transfers between devices, swap(): return lax.ppermute(value, axes, [(i, i ^ flip) for i in range(count)])  35.6 us
    ppermute x23, starting transfers between devices, swap(): return lax.ppermute(value, axes, [(i, i ^ flip) for i in range(count)])  24.5 us
    unnamed x13, local copies, waits for them, and re-layouts  3.24 us
    pallas_call x4, Pallas kernels, add_product(): kernel_call(functools.partial(weight_body, rows, mp_count, [0] + line, no...  3.13 us
    pallas_call x1, Pallas kernels, shards_gathered(): kernel_call(functools.partial(project_body, rows, mp_count), [struct((hal...  2.42 us
  transfers between devices with their start and end apart: 23, of which 13 were waited for; matrix products, arithmetic and copies ran while one was open for 2% of the time, Pallas kernels for 4%

commit v1 on v0

--- a/solution.py
+++ b/solution.py
@@ -13,7 +13,6 @@
 LANES = 128
 GATHER_BYTES = 8 << 20
 VMEM_BYTES = 40 << 20
-VMEM_ALL_BYTES = 62 << 20
 
 
 def unit_rows(values):
@@ -76,15 +75,19 @@
     return terms
 
 
-def kernel_call(body, outs, scratch=(), flops=0, vmem=VMEM_BYTES, **names):
+def kernel_call(body, outs, scratch=(), flops=0, **names):
     return pl.pallas_call(
         body,
         out_shape=outs,
         scratch_shapes=scratch,
-        compiler_params=pltpu.CompilerParams(vmem_limit_bytes=vmem),
+        compiler_params=pltpu.CompilerParams(vmem_limit_bytes=VMEM_BYTES),
         cost_estimate=pl.CostEstimate(flops=flops, bytes_accessed=1 << 20, transcendentals=0),
         **names,
     )
+
+
+def texts_body(texts_ref, out_ref):
+    out_ref[...] = unit_rows(texts_ref[...].astype(jnp.float32)).astype(jnp.bfloat16)
 
 
 def store_sums(extra_ref, column_sum, sum_row):
@@ -117,24 +120,14 @@
 
 
 def project_body(
-    rows, mp_count, place_ref, features_hbm, weight_hbm, texts_hbm,
-    keep_ref, send_ref, column_sum_ref, sum_row_ref, unit_txt_ref,
-    extra_ref, features_ref, weight_ref, texts_ref, arrived,
+    rows, mp_count, place_ref, features_ref, weight_ref,
+    keep_ref, send_ref, column_sum_ref, sum_row_ref, extra_ref,
 ):
-    copies = [
-        pltpu.make_async_copy(texts_hbm, texts_ref, arrived.at[0]),
-        pltpu.make_async_copy(features_hbm, features_ref, arrived.at[1]),
-        pltpu.make_async_copy(weight_hbm, weight_ref, arrived.at[2]),
-    ]
-    for copy in copies:
-        copy.start()
-    copies[0].wait()
-    unit_txt_ref[...] = unit_rows(texts_ref[...].astype(jnp.float32)).astype(jnp.bfloat16)
-    copies[1].wait()
     embed = weight_ref.shape[1]
     local_rows, width = features_ref.shape
     values = features_ref[...].astype(jnp.float32)
     row_sum = jnp.sum(values, axis=1, keepdims=True)
+    column_sum = jnp.sum(weight_ref[...].astype(jnp.float32), axis=0, keepdims=True)
     row = lax.broadcasted_iota(jnp.int32, (local_rows, LANES), 0)
     lane = lax.broadcasted_iota(jnp.int32, (local_rows, LANES), 1)
     sum_row = jnp.sum(jnp.where(row == lane, row_sum, 0.0), axis=0, keepdims=True)
@@ -144,8 +137,6 @@
         block = features_ref[pl.ds(start, rows), :].astype(jnp.float32)
         ordered.append(block - jnp.sum(block, axis=1, keepdims=True) / width)
     centred = jnp.concatenate(ordered, axis=0).astype(jnp.bfloat16)
-    copies[2].wait()
-    column_sum = jnp.sum(weight_ref[...].astype(jnp.float32), axis=0, keepdims=True)
     product = jnp.dot(centred, weight_ref[...], preferred_element_type=jnp.float32)
     half = local_rows // 2
     keep_ref[...] = product[:half]
@@ -294,7 +285,7 @@
     full_width = width * mp_count
     place = (lax.axis_index("dp") * mp_count + lax.axis_index("mp")).astype(jnp.int32).reshape(1)
     core, across, column = 1, 2, mp_count
-    line = list(range(count - plane_count, 0, -plane_count))
+    line = list(range(plane_count, count, plane_count))
 
     def swap(value, flip):
         return lax.ppermute(value, axes, [(i, i ^ flip) for i in range(count)])
@@ -310,28 +301,14 @@
     sums = [struct((1, embed), jnp.float32), struct((1, LANES), jnp.float32)]
     extra = pltpu.VMEM((rows, LANES), jnp.float32)
 
-    hbm = pl.BlockSpec(memory_space=pltpu.HBM)
-    keep, send, column_sum, sum_row, unit_txt_b = kernel_call(
+    keep, send, column_sum, sum_row = kernel_call(
         functools.partial(project_body, rows, mp_count),
-        [struct((half, embed), jnp.float32), struct((half, embed + LANES))]
-        + sums
-        + [struct(texts.shape)],
-        scratch=[
-            extra,
-            pltpu.VMEM(features.shape, features.dtype),
-            pltpu.VMEM(proj_weight.shape, proj_weight.dtype),
-            pltpu.VMEM(texts.shape, texts.dtype),
-            pltpu.SemaphoreType.DMA((3,)),
-        ],
-        in_specs=[smem, hbm, hbm, hbm],
+        [struct((half, embed), jnp.float32), struct((half, embed + LANES))] + sums,
+        scratch=[extra],
+        in_specs=[smem, vmem, vmem],
         flops=2 * local_rows * width * embed,
-        vmem=VMEM_ALL_BYTES,
         name="project",
-    )(place, features, proj_weight, texts)
-
-    texts_a = along_line(unit_txt_b)
-    texts_b = swap(texts_a, column)
-
+    )(place, features, proj_weight)
     own, send, column_sum, sum_row = kernel_call(
         functools.partial(chip_body, width, mp_count),
         [struct((rows, embed), jnp.float32), struct((rows, embed + LANES))] + sums,
@@ -339,6 +316,10 @@
         in_specs=[smem] + [vmem] * 4,
         name="chip_project",
     )(place, keep, swap(send, core), column_sum, sum_row)
+    unit_txt_b = kernel_call(texts_body, struct(texts.shape), name="unit_texts")(texts)
+    texts_a = along_line(unit_txt_b)
+    texts_b = swap(texts_a, column)
+
     unit_img_b, unit_img, inv_norm, normed_b, weight_sum = kernel_call(
         functools.partial(unit_body, full_width, mp_count),
         [
@@ -356,7 +337,7 @@
     images_a, texts_a, normed_b = lax.optimization_barrier((images_a, texts_a, normed_b))
     images_b = swap(images_a, core)
     normed_line, normed_order = normed_b, [0]
-    far, near = line[len(line) // 2], line[-1]
+    far, near = line[len(line) // 2], line[0]
     normed_line = jnp.concatenate([normed_line, swap(normed_line, far)], axis=0)
 
     keep, send = kernel_call(
@@ -413,12 +394,8 @@
         )
 
     grad_weight = add_product(0, [])
-    grads[2], grad_weight = lax.optimization_barrier((grads[2], grad_weight))
     others.append(swap(grads[2], core))
     grad_weight = add_product(1, [grad_weight])
-    grads[3], grad_weight, grad_features = lax.optimization_barrier(
-        (grads[3], grad_weight, grad_features)
-    )
     others.append(swap(grads[3], core))
     grad_weight = add_product(2, [grad_weight])
     grad_weight = add_product(3, [grad_weight])

time: 72.3 us -> 64.7 us (0.89)
  waiting for transfers between devices: 35.6 us -> 31.2 us
  starting transfers between devices: 24.5 us -> 22.5 us
  Pallas kernels: 7.81 us -> 5.91 us
    ppermute x23, waiting for transfers between devices: 35.6 us -> 31.2 us  [swap(): return lax.ppermute(value, axes, [(i, i ^ flip) for i in range(count)])]
    ppermute x23, starting transfers between devices: 24.5 us -> 22.5 us  [swap(): return lax.ppermute(value, axes, [(i, i ^ flip) for i in range(count)])]
    pallas_call x1, Pallas kernels: 2.42 us -> 0.41 us  [shards_gathered(): kernel_call(functools.partial(project_body, rows, mp_count), [struct((hal...]
    unnamed x13 -> x10, local copies, waits for them, and re-layouts: 3.24 us -> 3.84 us
  transfers between devices with their start and end apart: 23 -> 23, of which waited for: 13 -> 13; matrix products, arithmetic and copies ran while one was open for 2% -> 0% of each run, Pallas kernels for 4% -> 5%
where the time goes in v1:
time: 64.7 us; the launch traced here: 64.3 us
  waiting for transfers between devices  31.2 us (48%)
  starting transfers between devices  22.5 us (35%)
  Pallas kernels  5.91 us (9%)
  local copies, waits for them, and re-layouts  3.84 us (6%)
  between operations  0.8 us (1%)
    ppermute x23, waiting for transfers between devices, swap(): return lax.ppermute(value, axes, [(i, i ^ flip) for i in range(count)])  31.2 us
    ppermute x23, starting transfers between devices, swap(): return lax.ppermute(value, axes, [(i, i ^ flip) for i in range(count)])  22.5 us
    unnamed x10, local copies, waits for them, and re-layouts  3.84 us
    pallas_call x4, Pallas kernels, add_product(): kernel_call(functools.partial(weight_body, rows, mp_count, [0] + line, no...  3.13 us
  transfers between devices with their start and end apart: 23, of which 13 were waited for; matrix products, arithmetic and copies ran while one was open for 0% of the time, Pallas kernels for 5%

profile of v1, /device:TPU:0, one launch (start us, length us, event | category | flops | bytes accessed | tf_op | source)
XLA Modules:
  0.0 64.3 jit_solution(14167307298876169580)
XLA Ops:
  0.6 1.2 %copy-done = bf16[384,1152]{1,0:T(8,128)(2,1)S(1)} copy-done((bf16[384,1152]{1,0:T(8,128)(2,1)S(1)}, bf16[384,1152]{1,0:T(8,128)(2,1)}, u32[]{:S(2)}) %copy-start) | copy-done | bytes 884760
  3.6 1.0 %collective-permute-done.received_ref = bf16[64,1280]{1,0:T(8,128)(2,1)S(1)} collective-permute-done((bf16[64,1280]{1,0:T(8,128)(2,1)S(1)}, bf16[64,1280]{1,0:T(8,128)(2,1)S(1)}, u32[]{:S(2)}, u32[]{:S(2)}) %collective-permute-start) | collective-permute-done | bytes 163872 | tf_op jit(solution)/shard_map/ppermute | solution.py:291
  4.8 2.9 %collective-permute-start.1 = (bf16[32,1280]{1,0:T(8,128)(2,1)S(1)}, bf16[32,1280]{1,0:T(8,128)(2,1)S(1)}, u32[]{:S(2)}, u32[]{:S(2)}) collective-permute-start(bf16[32,1280]{1,0:T(8,128)(2,1)S(1)} %get-tuple-element.33), channel_id=1, source_target_pairs={{0,2},{1,3},{2,0},{3,1},{4,6},{5,7},{6,4},{7,5},{8,10},{9,11},{10,... | collective-permute-start | bytes 245768 | tf_op jit(solution)/shard_map/ppermute | solution.py:291
  8.8 1.6 %collective-permute-start.3 = (bf16[32,1152]{1,0:T(8,128)(2,1)S(1)}, bf16[32,1152]{1,0:T(8,128)(2,1)S(1)}, u32[]{:S(2)}, u32[]{:S(2)}) collective-permute-start(bf16[32,1152]{1,0:T(8,128)(2,1)S(1)} %unit_texts.1), channel_id=1, source_target_pairs={{0,8},{1,9},{2,10},{3,11},{4,12},{5,13},{6,14},{7,15},{8,0},{9,1},... | collective-permute-start | bytes 221192 | tf_op jit(solution)/shard_map/ppermute | solution.py:291
  10.4 2.6 %collective-permute-start.4 = (bf16[32,1152]{1,0:T(8,128)(2,1)S(1)}, bf16[32,1152]{1,0:T(8,128)(2,1)S(1)}, u32[]{:S(2)}, u32[]{:S(2)}) collective-permute-start(bf16[32,1152]{1,0:T(8,128)(2,1)S(1)} %unit_texts.1), channel_id=1, source_target_pairs={{0,16},{1,17},{2,18},{3,19},{4,20},{5,21},{6,22},{7,23},{8,24},{9,... | collective-permute-start | bytes 221192 | tf_op jit(solution)/shard_map/ppermute | solution.py:291
  13.2 0.9 %copy-done.3 = bf16[128,384]{1,0:T(8,128)(2,1)S(1)} copy-done((bf16[128,384]{1,0:T(8,128)(2,1)S(1)}, bf16[128,384]{1,0:T(8,128)(2,1)}, u32[]{:S(2)}) %copy-start.3) | copy-done | bytes 98328
  14.7 3.5 %collective-permute-done.4 = bf16[32,1152]{1,0:T(8,128)(2,1)S(1)} collective-permute-done((bf16[32,1152]{1,0:T(8,128)(2,1)S(1)}, bf16[32,1152]{1,0:T(8,128)(2,1)S(1)}, u32[]{:S(2)}, u32[]{:S(2)}) %collective-permute-start.4) | collective-permute-done | bytes 73760 | tf_op jit(solution)/shard_map/ppermute | solution.py:291
  18.2 1.0 %collective-permute-done.5 = bf16[32,1152]{1,0:T(8,128)(2,1)S(1)} collective-permute-done((bf16[32,1152]{1,0:T(8,128)(2,1)S(1)}, bf16[32,1152]{1,0:T(8,128)(2,1)S(1)}, u32[]{:S(2)}, u32[]{:S(2)}) %collective-permute-start.5) | collective-permute-done | bytes 73760 | tf_op jit(solution)/shard_map/ppermute | solution.py:291
  19.3 1.6 %collective-permute-start.7 = (bf16[128,1152]{1,0:T(8,128)(2,1)S(1)}, bf16[128,1152]{1,0:T(8,128)(2,1)S(1)}, u32[]{:S(2)}, u32[]{:S(2)}) collective-permute-start(bf16[128,1152]{1,0:T(8,128)(2,1)S(1)} %pad_maximum_fusion.1.texts_a_ref), channel_id=1, source_target_pairs={{0,4},{1,5},{2,6},{3,7},{4,0},{5,1},{6,2},{7,3},{8,12},{9,13},{10,... | collective-permute-start | bytes 884744 | tf_op jit(solution)/shard_map/ppermute | solution.py:291
  20.8 2.2 %collective-permute-start.8 = (bf16[128,384]{1,0:T(8,128)(2,1)S(1)}, bf16[128,384]{1,0:T(8,128)(2,1)S(1)}, u32[]{:S(2)}, u32[]{:S(2)}) collective-permute-start(bf16[128,384]{1,0:T(8,128)(2,1)S(1)} %get-tuple-element.45), channel_id=1, source_target_pairs={{0,16},{1,17},{2,18},{3,19},{4,20},{5,21},{6,22},{7,23},{8,24},{9,... | collective-permute-start | bytes 294920 | tf_op jit(solution)/shard_map/ppermute | solution.py:291
  23.0 4.4 %collective-permute-done.8 = bf16[128,384]{1,0:T(8,128)(2,1)S(1)} collective-permute-done((bf16[128,384]{1,0:T(8,128)(2,1)S(1)}, bf16[128,384]{1,0:T(8,128)(2,1)S(1)}, u32[]{:S(2)}, u32[]{:S(2)}) %collective-permute-start.8) | collective-permute-done | bytes 98336 | tf_op jit(solution)/shard_map/ppermute | solution.py:291
  28.6 1.4 %collective-permute-done.9.received_ref = bf16[64,1152]{1,0:T(8,128)(2,1)S(1)} collective-permute-done((bf16[64,1152]{1,0:T(8,128)(2,1)S(1)}, bf16[64,1152]{1,0:T(8,128)(2,1)S(1)}, u32[]{:S(2)}, u32[]{:S(2)}) %collective-permute-start.9) | collective-permute-done | bytes 147488 | tf_op jit(solution)/shard_map/ppermute | solution.py:291
  30.6 3.4 %collective-permute-done.11 = bf16[256,384]{1,0:T(8,128)(2,1)S(1)} collective-permute-done((bf16[256,384]{1,0:T(8,128)(2,1)S(1)}, bf16[256,384]{1,0:T(8,128)(2,1)S(1)}, u32[]{:S(2)}, u32[]{:S(2)}) %collective-permute-start.11) | collective-permute-done | bytes 196640 | tf_op jit(solution)/shard_map/ppermute | solution.py:291
  34.4 1.5 %collective-permute-start.15 = (bf16[512,384]{1,0:T(8,128)(2,1)S(1)}, bf16[512,384]{1,0:T(8,128)(2,1)S(1)}, u32[]{:S(2)}, u32[]{:S(2)}) collective-permute-start(bf16[512,384]{1,0:T(8,128)(2,1)S(1)} %pad_maximum_fusion.normed_ref), channel_id=1, source_target_pairs={{0,4},{1,5},{2,6},{3,7},{4,0},{5,1},{6,2},{7,3},{8,12},{9,13},{10,... | collective-permute-start | bytes 1179656 | tf_op jit(solution)/shard_map/ppermute | solution.py:291
  36.9 2.8 %collective-permute-start.13 = (bf16[32,1152]{1,0:T(8,128)(2,1)S(1)}, bf16[32,1152]{1,0:T(8,128)(2,1)S(1)}, u32[]{:S(2)}, u32[]{:S(2)}) collective-permute-start(bf16[32,1152]{1,0:T(8,128)(2,1)S(1)} %grad_project.1), channel_id=1, source_target_pairs={{0,16},{1,17},{2,18},{3,19},{4,20},{5,21},{6,22},{7,23},{8,24},{9,... | collective-permute-start | bytes 221192 | tf_op jit(solution)/shard_map/ppermute | solution.py:291
  39.6 0.9 %collective-permute-start.14 = (bf16[32,1152]{1,0:T(8,128)(2,1)S(1)}, bf16[32,1152]{1,0:T(8,128)(2,1)S(1)}, u32[]{:S(2)}, u32[]{:S(2)}) collective-permute-start(bf16[32,1152]{1,0:T(8,128)(2,1)S(1)} %grad_project.1), channel_id=1, source_target_pairs={{0,24},{1,25},{2,26},{3,27},{4,28},{5,29},{6,30},{7,31},{8,16},{9,... | collective-permute-start | bytes 221192 | tf_op jit(solution)/shard_map/ppermute | solution.py:291
  40.6 3.2 %collective-permute-done.13 = bf16[32,1152]{1,0:T(8,128)(2,1)S(1)} collective-permute-done((bf16[32,1152]{1,0:T(8,128)(2,1)S(1)}, bf16[32,1152]{1,0:T(8,128)(2,1)S(1)}, u32[]{:S(2)}, u32[]{:S(2)}) %collective-permute-start.13) | collective-permute-done | bytes 73760 | tf_op jit(solution)/shard_map/ppermute | solution.py:291
  43.8 2.0 %collective-permute-done.14 = bf16[32,1152]{1,0:T(8,128)(2,1)S(1)} collective-permute-done((bf16[32,1152]{1,0:T(8,128)(2,1)S(1)}, bf16[32,1152]{1,0:T(8,128)(2,1)S(1)}, u32[]{:S(2)}, u32[]{:S(2)}) %collective-permute-start.14) | collective-permute-done | bytes 73760 | tf_op jit(solution)/shard_map/ppermute | solution.py:291
  47.0 2.3 %collective-permute-start.19 = (bf16[128,1152]{1,0:T(8,128)(2,1)S(1)}, bf16[128,1152]{1,0:T(8,128)(2,1)S(1)}, u32[]{:S(2)}, u32[]{:S(2)}) collective-permute-start(bf16[128,1152]{1,0:T(8,128)(2,1)S(1)} %pad_maximum_fusion.2.refs_0_.own_ref), channel_id=1, source_target_pairs={{0,6},{1,7},{2,4},{3,5},{4,2},{5,3},{6,0},{7,1},{8,14},{9,15},{10,... | collective-permute-start | bytes 884744 | tf_op jit(solution)/shard_map/ppermute | solution.py:291
  49.4 5.6 %collective-permute-done.17.refs_2_.own_ref = bf16[128,1152]{1,0:T(8,128)(2,1)S(1)} collective-permute-done((bf16[128,1152]{1,0:T(8,128)(2,1)S(1)}, bf16[128,1152]{1,0:T(8,128)(2,1)S(1)}, u32[]{:S(2)}, u32[]{:S(2)}) %collective-permute-start.17) | collective-permute-done | bytes 294944 | tf_op jit(solution)/shard_map/ppermute | solution.py:291
  55.0 1.0 %collective-permute-done.21.own_ref = bf16[128,1152]{1,0:T(8,128)(2,1)S(1)} collective-permute-done((bf16[128,1152]{1,0:T(8,128)(2,1)S(1)}, bf16[128,1152]{1,0:T(8,128)(2,1)S(1)}, u32[]{:S(2)}, u32[]{:S(2)}) %collective-permute-start.21) | collective-permute-done | bytes 294944 | tf_op jit(solution)/shard_map/ppermute | solution.py:291
  56.0 4.1 %collective-permute-done.19.own_ref = bf16[128,1152]{1,0:T(8,128)(2,1)S(1)} collective-permute-done((bf16[128,1152]{1,0:T(8,128)(2,1)S(1)}, bf16[128,1152]{1,0:T(8,128)(2,1)S(1)}, u32[]{:S(2)}, u32[]{:S(2)}) %collective-permute-start.19) | collective-permute-done | bytes 294944 | tf_op jit(solution)/shard_map/ppermute | solution.py:291
  60.6 1.1 %grad_features.1 = bf16[128,384]{1,0:T(8,128)(2,1)} custom-call(s32[1]{0:T(128)} %bitcast.place_ref, bf16[384,1152]{1,0:T(8,128)(2,1)S(1)} %copy-done.1, f32[1,1152]{1,0:T(1,128)S(1)} %get-tuple-element.36.weight_sum_ref, bf16[128,1152]{1,0:T(8,128)(2,1)S(1)} %pad_maximum_fusion.2.refs_0_.own_ref, ...), custom_call_target="tpu_custom_call" | custom-call | flops 113246208 | bytes 1048576 | tf_op jit(solution)/shard_map/grad_features/pallas_call | solution.py:370
  62.7 1.7 %weight.7 = f32[384,1152]{1,0:T(8,128)} custom-call(s32[1]{0:T(128)} %bitcast.place_ref, bf16[512,384]{1,0:T(8,128)(2,1)S(1)} %collective-permute-done.15.normed_ref, bf16[128,1152]{1,0:T(8,128)(2,1)S(1)} %collective-permute-done.19.own_ref, bf16[128,1152]{1,0:T(8,128)(2,1)S(1)} %collective-permute-done.20.other_ref, f32[384,1152]{1,0:T(8,128)S(1)} %weight.6.refs_0_), custom_call_target="tpu_custom_call" | custom-call | flops 226492416 | bytes 1048576 | tf_op jit(solution)/shard_map/weight/pallas_call | solution.py:380
  (49 shorter events, 9.7 us)
Async XLA Ops:
  3.1 1.5 %collective-permute-start = (bf16[64,1280]{1,0:T(8,128)(2,1)S(1)}, bf16[64,1280]{1,0:T(8,128)(2,1)S(1)}, u32[]{:S(2)}, u32[]{:S(2)}) collective-permute-start(bf16[64,1280]{1,0:T(8,128)(2,1)S(1)} %get-tuple-element.29), channel_id=1, source_target_pairs={{0,1},{1,0},{2,3},{3,2},{4,5},{5,4},{6,7},{7,6},{8,9},{9,8},{10,11... | collective-permute-start | bytes 491528 | tf_op jit(solution)/shard_map/ppermute | solution.py:291
  4.8 8.4 %collective-permute-start.1 = (bf16[32,1280]{1,0:T(8,128)(2,1)S(1)}, bf16[32,1280]{1,0:T(8,128)(2,1)S(1)}, u32[]{:S(2)}, u32[]{:S(2)}) collective-permute-start(bf16[32,1280]{1,0:T(8,128)(2,1)S(1)} %get-tuple-element.33), channel_id=1, source_target_pairs={{0,2},{1,3},{2,0},{3,1},{4,6},{5,7},{6,4},{7,5},{8,10},{9,11},{10,... | collective-permute-start | bytes 245768 | tf_op jit(solution)/shard_map/ppermute | solution.py:291
  8.8 5.9 %collective-permute-start.3 = (bf16[32,1152]{1,0:T(8,128)(2,1)S(1)}, bf16[32,1152]{1,0:T(8,128)(2,1)S(1)}, u32[]{:S(2)}, u32[]{:S(2)}) collective-permute-start(bf16[32,1152]{1,0:T(8,128)(2,1)S(1)} %unit_texts.1), channel_id=1, source_target_pairs={{0,8},{1,9},{2,10},{3,11},{4,12},{5,13},{6,14},{7,15},{8,0},{9,1},... | collective-permute-start | bytes 221192 | tf_op jit(solution)/shard_map/ppermute | solution.py:291
  10.4 7.8 %collective-permute-start.4 = (bf16[32,1152]{1,0:T(8,128)(2,1)S(1)}, bf16[32,1152]{1,0:T(8,128)(2,1)S(1)}, u32[]{:S(2)}, u32[]{:S(2)}) collective-permute-start(bf16[32,1152]{1,0:T(8,128)(2,1)S(1)} %unit_texts.1), channel_id=1, source_target_pairs={{0,16},{1,17},{2,18},{3,19},{4,20},{5,21},{6,22},{7,23},{8,24},{9,... | collective-permute-start | bytes 221192 | tf_op jit(solution)/shard_map/ppermute | solution.py:291
  13.0 6.3 %collective-permute-start.5 = (bf16[32,1152]{1,0:T(8,128)(2,1)S(1)}, bf16[32,1152]{1,0:T(8,128)(2,1)S(1)}, u32[]{:S(2)}, u32[]{:S(2)}) collective-permute-start(bf16[32,1152]{1,0:T(8,128)(2,1)S(1)} %unit_texts.1), channel_id=1, source_target_pairs={{0,24},{1,25},{2,26},{3,27},{4,28},{5,29},{6,30},{7,31},{8,16},{9,... | collective-permute-start | bytes 221192 | tf_op jit(solution)/shard_map/ppermute | solution.py:291
  14.3 6.5 %collective-permute-start.2 = (bf16[32,1152]{1,0:T(8,128)(2,1)S(1)}, bf16[32,1152]{1,0:T(8,128)(2,1)S(1)}, u32[]{:S(2)}, u32[]{:S(2)}) collective-permute-start(bf16[32,1152]{1,0:T(8,128)(2,1)S(1)} %get-tuple-element.39), channel_id=1, source_target_pairs={{0,2},{1,3},{2,0},{3,1},{4,6},{5,7},{6,4},{7,5},{8,10},{9,11},{10,... | collective-permute-start | bytes 221192 | tf_op jit(solution)/shard_map/ppermute | solution.py:291
  19.3 8.2 %collective-permute-start.7 = (bf16[128,1152]{1,0:T(8,128)(2,1)S(1)}, bf16[128,1152]{1,0:T(8,128)(2,1)S(1)}, u32[]{:S(2)}, u32[]{:S(2)}) collective-permute-start(bf16[128,1152]{1,0:T(8,128)(2,1)S(1)} %pad_maximum_fusion.1.texts_a_ref), channel_id=1, source_target_pairs={{0,4},{1,5},{2,6},{3,7},{4,0},{5,1},{6,2},{7,3},{8,12},{9,13},{10,... | collective-permute-start | bytes 884744 | tf_op jit(solution)/shard_map/ppermute | solution.py:291
  20.8 6.6 %collective-permute-start.8 = (bf16[128,384]{1,0:T(8,128)(2,1)S(1)}, bf16[128,384]{1,0:T(8,128)(2,1)S(1)}, u32[]{:S(2)}, u32[]{:S(2)}) collective-permute-start(bf16[128,384]{1,0:T(8,128)(2,1)S(1)} %get-tuple-element.45), channel_id=1, source_target_pairs={{0,16},{1,17},{2,18},{3,19},{4,20},{5,21},{6,22},{7,23},{8,24},{9,... | collective-permute-start | bytes 294920 | tf_op jit(solution)/shard_map/ppermute | solution.py:291
  23.0 4.5 %collective-permute-start.6 = (bf16[64,1152]{1,0:T(8,128)(2,1)S(1)}, bf16[64,1152]{1,0:T(8,128)(2,1)S(1)}, u32[]{:S(2)}, u32[]{:S(2)}) collective-permute-start(bf16[64,1152]{1,0:T(8,128)(2,1)S(1)} %pad_maximum_fusion.4.images_a_ref), channel_id=1, source_target_pairs={{0,1},{1,0},{2,3},{3,2},{4,5},{5,4},{6,7},{7,6},{8,9},{9,8},{10,11... | collective-permute-start | bytes 442376 | tf_op jit(solution)/shard_map/ppermute | solution.py:291
  28.2 5.7 %collective-permute-start.11 = (bf16[256,384]{1,0:T(8,128)(2,1)S(1)}, bf16[256,384]{1,0:T(8,128)(2,1)S(1)}, u32[]{:S(2)}, u32[]{:S(2)}) collective-permute-start(bf16[256,384]{1,0:T(8,128)(2,1)S(1)} %pad_maximum_fusion.3), channel_id=1, source_target_pairs={{0,8},{1,9},{2,10},{3,11},{4,12},{5,13},{6,14},{7,15},{8,0},{9,1},... | collective-permute-start | bytes 589832 | tf_op jit(solution)/shard_map/ppermute | solution.py:291
  28.6 1.4 %collective-permute-start.9 = (bf16[64,1152]{1,0:T(8,128)(2,1)S(1)}, bf16[64,1152]{1,0:T(8,128)(2,1)S(1)}, u32[]{:S(2)}, u32[]{:S(2)}) collective-permute-start(bf16[64,1152]{1,0:T(8,128)(2,1)S(1)} %get-tuple-element.46), channel_id=1, source_target_pairs={{0,1},{1,0},{2,3},{3,2},{4,5},{5,4},{6,7},{7,6},{8,9},{9,8},{10,11... | collective-permute-start | bytes 442376 | tf_op jit(solution)/shard_map/ppermute | solution.py:291
  30.0 4.4 %collective-permute-start.10 = (bf16[32,1152]{1,0:T(8,128)(2,1)S(1)}, bf16[32,1152]{1,0:T(8,128)(2,1)S(1)}, u32[]{:S(2)}, u32[]{:S(2)}) collective-permute-start(bf16[32,1152]{1,0:T(8,128)(2,1)S(1)} %get-tuple-element.48), channel_id=1, source_target_pairs={{0,2},{1,3},{2,0},{3,1},{4,6},{5,7},{6,4},{7,5},{8,10},{9,11},{10,... | collective-permute-start | bytes 221192 | tf_op jit(solution)/shard_map/ppermute | solution.py:291
  34.4 11.4 %collective-permute-start.15 = (bf16[512,384]{1,0:T(8,128)(2,1)S(1)}, bf16[512,384]{1,0:T(8,128)(2,1)S(1)}, u32[]{:S(2)}, u32[]{:S(2)}) collective-permute-start(bf16[512,384]{1,0:T(8,128)(2,1)S(1)} %pad_maximum_fusion.normed_ref), channel_id=1, source_target_pairs={{0,4},{1,5},{2,6},{3,7},{4,0},{5,1},{6,2},{7,3},{8,12},{9,13},{10,... | collective-permute-start | bytes 1179656 | tf_op jit(solution)/shard_map/ppermute | solution.py:291
  36.1 24.5 %copy-start.1 = (bf16[384,1152]{1,0:T(8,128)(2,1)S(1)}, bf16[384,1152]{1,0:T(8,128)(2,1)}, u32[]{:S(2)}) copy-start(bf16[384,1152]{1,0:T(8,128)(2,1)} %weight_ref.3) | copy-start | bytes 2654212
  36.1 4.5 %collective-permute-start.12 = (bf16[32,1152]{1,0:T(8,128)(2,1)S(1)}, bf16[32,1152]{1,0:T(8,128)(2,1)S(1)}, u32[]{:S(2)}, u32[]{:S(2)}) collective-permute-start(bf16[32,1152]{1,0:T(8,128)(2,1)S(1)} %grad_project.1), channel_id=1, source_target_pairs={{0,8},{1,9},{2,10},{3,11},{4,12},{5,13},{6,14},{7,15},{8,0},{9,1},... | collective-permute-start | bytes 221192 | tf_op jit(solution)/shard_map/ppermute | solution.py:291
  36.9 6.9 %collective-permute-start.13 = (bf16[32,1152]{1,0:T(8,128)(2,1)S(1)}, bf16[32,1152]{1,0:T(8,128)(2,1)S(1)}, u32[]{:S(2)}, u32[]{:S(2)}) collective-permute-start(bf16[32,1152]{1,0:T(8,128)(2,1)S(1)} %grad_project.1), channel_id=1, source_target_pairs={{0,16},{1,17},{2,18},{3,19},{4,20},{5,21},{6,22},{7,23},{8,24},{9,... | collective-permute-start | bytes 221192 | tf_op jit(solution)/shard_map/ppermute | solution.py:291
  39.6 6.2 %collective-permute-start.14 = (bf16[32,1152]{1,0:T(8,128)(2,1)S(1)}, bf16[32,1152]{1,0:T(8,128)(2,1)S(1)}, u32[]{:S(2)}, u32[]{:S(2)}) collective-permute-start(bf16[32,1152]{1,0:T(8,128)(2,1)S(1)} %grad_project.1), channel_id=1, source_target_pairs={{0,24},{1,25},{2,26},{3,27},{4,28},{5,29},{6,30},{7,31},{8,16},{9,... | collective-permute-start | bytes 221192 | tf_op jit(solution)/shard_map/ppermute | solution.py:291
  45.8 9.2 %collective-permute-start.17 = (bf16[128,1152]{1,0:T(8,128)(2,1)S(1)}, bf16[128,1152]{1,0:T(8,128)(2,1)S(1)}, u32[]{:S(2)}, u32[]{:S(2)}) collective-permute-start(bf16[128,1152]{1,0:T(8,128)(2,1)S(1)} %pad_maximum_fusion.2.refs_0_.own_ref), channel_id=1, source_target_pairs={{0,2},{1,3},{2,0},{3,1},{4,6},{5,7},{6,4},{7,5},{8,10},{9,11},{10,... | collective-permute-start | bytes 884744 | tf_op jit(solution)/shard_map/ppermute | solution.py:291
  46.4 9.6 %collective-permute-start.21 = (bf16[128,1152]{1,0:T(8,128)(2,1)S(1)}, bf16[128,1152]{1,0:T(8,128)(2,1)S(1)}, u32[]{:S(2)}, u32[]{:S(2)}) collective-permute-start(bf16[128,1152]{1,0:T(8,128)(2,1)S(1)} %pad_maximum_fusion.2.refs_0_.own_ref), channel_id=1, source_target_pairs={{0,4},{1,5},{2,6},{3,7},{4,0},{5,1},{6,2},{7,3},{8,12},{9,13},{10,... | collective-permute-start | bytes 884744 | tf_op jit(solution)/shard_map/ppermute | solution.py:291
  47.0 13.0 %collective-permute-start.19 = (bf16[128,1152]{1,0:T(8,128)(2,1)S(1)}, bf16[128,1152]{1,0:T(8,128)(2,1)S(1)}, u32[]{:S(2)}, u32[]{:S(2)}) collective-permute-start(bf16[128,1152]{1,0:T(8,128)(2,1)S(1)} %pad_maximum_fusion.2.refs_0_.own_ref), channel_id=1, source_target_pairs={{0,6},{1,7},{2,4},{3,5},{4,2},{5,3},{6,0},{7,1},{8,14},{9,15},{10,... | collective-permute-start | bytes 884744 | tf_op jit(solution)/shard_map/ppermute | solution.py:291
  49.4 10.7 %collective-permute-start.16 = (bf16[128,1152]{1,0:T(8,128)(2,1)S(1)}, bf16[128,1152]{1,0:T(8,128)(2,1)S(1)}, u32[]{:S(2)}, u32[]{:S(2)}) collective-permute-start(bf16[128,1152]{1,0:T(8,128)(2,1)S(1)} %pad_maximum_fusion.2.refs_0_.own_ref), channel_id=1, source_target_pairs={{0,1},{1,0},{2,3},{3,2},{4,5},{5,4},{6,7},{7,6},{8,9},{9,8},{10,11... | collective-permute-start | bytes 884744 | tf_op jit(solution)/shard_map/ppermute | solution.py:291
  55.0 5.6 %collective-permute-start.18 = (bf16[128,1152]{1,0:T(8,128)(2,1)S(1)}, bf16[128,1152]{1,0:T(8,128)(2,1)S(1)}, u32[]{:S(2)}, u32[]{:S(2)}) collective-permute-start(bf16[128,1152]{1,0:T(8,128)(2,1)S(1)} %collective-permute-done.17.refs_2_.own_ref), channel_id=1, source_target_pairs={{0,1},{1,0},{2,3},{3,2},{4,5},{5,4},{6,7},{7,6},{8,9},{9,8},{10,11... | collective-permute-start | bytes 884744 | tf_op jit(solution)/shard_map/ppermute | solution.py:291
  55.9 6.2 %collective-permute-start.22 = (bf16[128,1152]{1,0:T(8,128)(2,1)S(1)}, bf16[128,1152]{1,0:T(8,128)(2,1)S(1)}, u32[]{:S(2)}, u32[]{:S(2)}) collective-permute-start(bf16[128,1152]{1,0:T(8,128)(2,1)S(1)} %collective-permute-done.21.own_ref), channel_id=1, source_target_pairs={{0,1},{1,0},{2,3},{3,2},{4,5},{5,4},{6,7},{7,6},{8,9},{9,8},{10,11... | collective-permute-start | bytes 884744 | tf_op jit(solution)/shard_map/ppermute | solution.py:291
  60.1 2.6 %collective-permute-start.20 = (bf16[128,1152]{1,0:T(8,128)(2,1)S(1)}, bf16[128,1152]{1,0:T(8,128)(2,1)S(1)}, u32[]{:S(2)}, u32[]{:S(2)}) collective-permute-start(bf16[128,1152]{1,0:T(8,128)(2,1)S(1)} %collective-permute-done.19.own_ref), channel_id=1, source_target_pairs={{0,1},{1,0},{2,3},{3,2},{4,5},{5,4},{6,7},{7,6},{8,9},{9,8},{10,11... | collective-permute-start | bytes 884744 | tf_op jit(solution)/shard_map/ppermute | solution.py:291
  (4 other events, 3.8 us)

commit v2 on v1

--- a/solution.py
+++ b/solution.py
@@ -81,7 +81,7 @@
         out_shape=outs,
         scratch_shapes=scratch,
         compiler_params=pltpu.CompilerParams(vmem_limit_bytes=VMEM_BYTES),
-        cost_estimate=pl.CostEstimate(flops=flops, bytes_accessed=1 << 20, transcendentals=0),
+        cost_estimate=pl.CostEstimate(flops=flops, bytes_accessed=0, transcendentals=0),
         **names,
     )
 
@@ -176,8 +176,8 @@
 
 
 def unit_body(
-    full_width, mp_count, place_ref, features_ref, own_ref, received_ref, column_sum_ref,
-    sum_row_ref, unit_b_ref, unit_ref, inv_norm_ref, normed_ref, weight_sum_ref,
+    full_width, mp_count, place_ref, own_ref, received_ref, column_sum_ref, sum_row_ref,
+    unit_b_ref, unit_ref, inv_norm_ref, mean_ref, weight_sum_ref,
 ):
     rows, embed = own_ref.shape
     columns = [column_sum_ref[...], None]
@@ -195,9 +195,13 @@
     unit_ref[...] = unit_img
     unit_b_ref[...] = unit_img.astype(jnp.bfloat16)
     inv_norm_ref[...] = inv_norm
-    mean = pick_rows(full_row, features_ref.shape[0], 0) / full_width
-    normed_ref[...] = (features_ref[...].astype(jnp.float32) - mean).astype(jnp.bfloat16)
+    mean_ref[...] = pick_rows(full_row, mean_ref.shape[0], 0) / full_width
     weight_sum_ref[...] = columns[0] + columns[1]
+
+
+def centre_body(features_ref, mean_ref, out_ref):
+    centred = features_ref[...].astype(jnp.float32) - mean_ref[...]
+    out_ref[...] = centred.astype(jnp.bfloat16)
 
 
 def slopes_body(images_a_ref, images_b_ref, texts_a_ref, texts_b_ref, keep_ref, send_ref):
@@ -240,13 +244,12 @@
     out_ref[...] = grad_proj.astype(jnp.bfloat16)
 
 
-def weight_body(rows, mp_count, line, normed_order, flip, place_ref, normed_ref, own_ref, other_ref,
-                *refs):
+def weight_body(rows, mp_count, normed_order, order, flip, place_ref, normed_ref, own_ref, other_ref, *refs):
     (*previous, out_ref) = refs
     blocks = []
     for i in range(2):
         group = (place_ref[0] ^ flip ^ i) & (mp_count - 1)
-        for line_flip in line:
+        for line_flip in order:
             start = (normed_order.index(line_flip) * mp_count + group) * rows
             blocks.append(normed_ref[pl.ds(pl.multiple_of(start, rows), rows), :])
     total = lax.dot_general(
@@ -293,8 +296,8 @@
     def struct(dims, kind=jnp.bfloat16):
         return jax.ShapeDtypeStruct(dims, kind)
 
-    def along_line(value):
-        return jnp.concatenate([value] + [swap(value, flip) for flip in line], axis=0)
+    def along_line(value, order):
+        return jnp.concatenate([value] + [swap(value, flip) for flip in order], axis=0)
 
     smem = pl.BlockSpec(memory_space=pltpu.SMEM)
     vmem = pl.BlockSpec(memory_space=pltpu.VMEM)
@@ -317,28 +320,28 @@
         name="chip_project",
     )(place, keep, swap(send, core), column_sum, sum_row)
     unit_txt_b = kernel_call(texts_body, struct(texts.shape), name="unit_texts")(texts)
-    texts_a = along_line(unit_txt_b)
+    texts_a = along_line(unit_txt_b, line[::-1])
     texts_b = swap(texts_a, column)
 
-    unit_img_b, unit_img, inv_norm, normed_b, weight_sum = kernel_call(
+    unit_img_b, unit_img, inv_norm, mean, weight_sum = kernel_call(
         functools.partial(unit_body, full_width, mp_count),
         [
             struct((rows, embed)),
             struct((rows, embed), jnp.float32),
             struct((rows, 1), jnp.float32),
-            struct((local_rows, width)),
+            struct((local_rows, 1), jnp.float32),
             struct((1, embed), jnp.float32),
         ],
-        in_specs=[smem] + [vmem] * 5,
+        in_specs=[smem] + [vmem] * 4,
         name="unit_images",
-    )(place, features, own, swap(send, across), column_sum, sum_row)
+    )(place, own, swap(send, across), column_sum, sum_row)
+    normed_b = kernel_call(centre_body, struct(features.shape), name="centre")(features, mean)
 
     images_a = jnp.concatenate([unit_img_b, swap(unit_img_b, across)], axis=0)
-    images_a, texts_a, normed_b = lax.optimization_barrier((images_a, texts_a, normed_b))
+    images_a, normed_b = lax.optimization_barrier((images_a, normed_b))
     images_b = swap(images_a, core)
-    normed_line, normed_order = normed_b, [0]
-    far, near = line[len(line) // 2], line[0]
-    normed_line = jnp.concatenate([normed_line, swap(normed_line, far)], axis=0)
+    normed_order = [0] + line[::-1]
+    normed_parts = [normed_b] + [swap(normed_b, flip) for flip in normed_order[1:]]
 
     keep, send = kernel_call(
         slopes_body,
@@ -346,40 +349,34 @@
         flops=4 * local_rows * local_rows * 2 * embed,
         name="slopes",
     )(images_a, images_b, texts_a, texts_b)
-    send, normed_line = lax.optimization_barrier((send, normed_line))
-    normed_line = jnp.concatenate([normed_line, swap(normed_line, near)], axis=0)
-    normed_order = [0, far, near, far ^ near]
+    at8, at16 = normed_order.index(line[0]), normed_order.index(line[1])
+    send, normed_parts[at8], normed_parts[at16] = lax.optimization_barrier(
+        (send, normed_parts[at8], normed_parts[at16])
+    )
     own, send = kernel_call(
         chip_grad_body,
         [struct((rows, embed), jnp.float32), struct((rows, embed))],
         name="chip_grad",
     )(keep, swap(send, core))
     received = swap(send, across)
-    received, normed_line = lax.optimization_barrier((received, normed_line))
+    received, *normed_parts = lax.optimization_barrier((received, *normed_parts))
+    normed_line = jnp.concatenate(normed_parts, axis=0)
     normed_other = swap(normed_line, column)
     grad_rows = kernel_call(grad_body, struct((rows, embed)), name="grad_project")(
         unit_img, inv_norm, own, received
     )
 
-    grad_line = along_line(grad_rows)
+    grad_order = [0] + line[::-1]
+    grad_line = along_line(grad_rows, grad_order[1:])
     grad_line, normed_other = lax.optimization_barrier((grad_line, normed_other))
     plane = [0, across, column, column | across]
     grads = [grad_line] + [swap(grad_line, flip) for flip in plane[1:]]
-    others = [swap(value, core) for value in grads[:2]]
-    group = [grads[0], others[0], grads[1], others[1]]
-    grad_features = kernel_call(
-        functools.partial(features_body, full_width, rows, mp_count),
-        struct(features.shape),
-        scratch=[pltpu.VMEM((local_rows, embed), jnp.bfloat16)],
-        in_specs=[smem] + [vmem] * (2 + mp_count),
-        flops=2 * local_rows * width * embed,
-        name="grad_features",
-    )(place, proj_weight, weight_sum, *group)
-
+    y_at = plane.index(across)
+    others = [swap(grads[0], core)]
     def add_product(index, previous):
         return kernel_call(
             functools.partial(
-                weight_body, rows, mp_count, [0] + line, normed_order, plane[index]
+                weight_body, rows, mp_count, normed_order, grad_order, plane[index]
             ),
             struct(proj_weight.shape, jnp.float32),
             in_specs=[smem] + [vmem] * (3 + len(previous)),
@@ -393,12 +390,27 @@
             *previous,
         )
 
-    grad_weight = add_product(0, [])
-    others.append(swap(grads[2], core))
-    grad_weight = add_product(1, [grad_weight])
-    others.append(swap(grads[3], core))
-    grad_weight = add_product(2, [grad_weight])
-    grad_weight = add_product(3, [grad_weight])
+    grad_weight = first_weight = add_product(0, [])
+    others_y = None
+    grad_y, _ = lax.optimization_barrier((grads[y_at], first_weight))
+    others_y = swap(grad_y, core)
+    grad_features = kernel_call(
+        functools.partial(features_body, full_width, rows, mp_count),
+        struct(features.shape),
+        scratch=[pltpu.VMEM((local_rows, embed), jnp.bfloat16)],
+        in_specs=[smem] + [vmem] * (2 + mp_count),
+        name="grad_features",
+    )(place, proj_weight, weight_sum, grads[0], others[0], grads[y_at], others_y)
+
+    for i in range(1, 4):
+        if plane[i] == across:
+            others.append(others_y)
+        else:
+            grads[i], _ = lax.optimization_barrier((grads[i], first_weight))
+            if i == 3:
+                grads[i], grad_features = lax.optimization_barrier((grads[i], grad_features))
+            others.append(swap(grads[i], core))
+        grad_weight = add_product(i, [grad_weight])
     return grad_features, grad_weight
 
 

time: 64.7 us -> 69 us (1.066)
  waiting for transfers between devices: 31.2 us -> 35.1 us
  starting transfers between devices: 22.5 us -> 23.8 us
  local copies, waits for them, and re-layouts: 3.84 us -> 3.02 us
    ppermute x23 -> x24, waiting for transfers between devices: 31.2 us -> 35.1 us  [swap(): return lax.ppermute(value, axes, [(i, i ^ flip) for i in range(count)])]
    ppermute x23 -> x24, starting transfers between devices: 22.5 us -> 23.8 us  [swap(): return lax.ppermute(value, axes, [(i, i ^ flip) for i in range(count)])]
    unnamed x10 -> x13, local copies, waits for them, and re-layouts: 3.84 us -> 3 us
    pallas_call x4 -> x5, Pallas kernels: 3.13 us -> 3.2 us  [the longest x4 3.12 us: add_product(): kernel_call(functools.partial(weight_body, rows, mp_count, normed_order,...]
  transfers between devices with their start and end apart: 23 -> 24, of which waited for: 13 -> 14; matrix products, arithmetic and copies ran while one was open for 0% -> 0% of each run, Pallas kernels for 5% -> 5%
where the time goes in v2:
time: 69 us; the launch traced here: 68.8 us
  waiting for transfers between devices  35.1 us (51%)
  starting transfers between devices  23.8 us (34%)
  Pallas kernels  5.98 us (9%)
  local copies, waits for them, and re-layouts  3.02 us (4%)
  between operations  0.8 us (1%)
    ppermute x24, waiting for transfers between devices, swap(): return lax.ppermute(value, axes, [(i, i ^ flip) for i in range(count)])  35.1 us
    ppermute x24, starting transfers between devices, swap(): return lax.ppermute(value, axes, [(i, i ^ flip) for i in range(count)])  23.8 us
    pallas_call x4, Pallas kernels, add_product(): kernel_call(functools.partial(weight_body, rows, mp_count, normed_order,...  3.12 us
    unnamed x13, local copies, waits for them, and re-layouts  3 us
  transfers between devices with their start and end apart: 24, of which 14 were waited for; matrix products, arithmetic and copies ran while one was open for 0% of the time, Pallas kernels for 5%

profile of v2, /device:TPU:0, one launch (start us, length us, event | category | flops | bytes accessed | tf_op | source)
XLA Modules:
  0.0 68.8 jit_solution(2616299447368782807)
XLA Ops:
  0.6 1.2 %copy-done = bf16[384,1152]{1,0:T(8,128)(2,1)S(1)} copy-done((bf16[384,1152]{1,0:T(8,128)(2,1)S(1)}, bf16[384,1152]{1,0:T(8,128)(2,1)}, u32[]{:S(2)}) %copy-start) | copy-done | bytes 884760
  3.6 1.0 %collective-permute-done.received_ref = bf16[64,1280]{1,0:T(8,128)(2,1)S(1)} collective-permute-done((bf16[64,1280]{1,0:T(8,128)(2,1)S(1)}, bf16[64,1280]{1,0:T(8,128)(2,1)S(1)}, u32[]{:S(2)}, u32[]{:S(2)}) %collective-permute-start) | collective-permute-done | bytes 163872 | tf_op jit(solution)/shard_map/ppermute | solution.py:294
  4.8 3.0 %collective-permute-start.1 = (bf16[32,1280]{1,0:T(8,128)(2,1)S(1)}, bf16[32,1280]{1,0:T(8,128)(2,1)S(1)}, u32[]{:S(2)}, u32[]{:S(2)}) collective-permute-start(bf16[32,1280]{1,0:T(8,128)(2,1)S(1)} %get-tuple-element.41), channel_id=1, source_target_pairs={{0,2},{1,3},{2,0},{3,1},{4,6},{5,7},{6,4},{7,5},{8,10},{9,11},{10,... | collective-permute-start | bytes 245768 | tf_op jit(solution)/shard_map/ppermute | solution.py:294
  8.8 1.6 %collective-permute-start.6 = (bf16[32,1152]{1,0:T(8,128)(2,1)S(1)}, bf16[32,1152]{1,0:T(8,128)(2,1)S(1)}, u32[]{:S(2)}, u32[]{:S(2)}) collective-permute-start(bf16[32,1152]{1,0:T(8,128)(2,1)S(1)} %unit_texts.1), channel_id=1, source_target_pairs={{0,8},{1,9},{2,10},{3,11},{4,12},{5,13},{6,14},{7,15},{8,0},{9,1},... | collective-permute-start | bytes 221192 | tf_op jit(solution)/shard_map/ppermute | solution.py:294
  10.4 2.6 %collective-permute-start.5 = (bf16[32,1152]{1,0:T(8,128)(2,1)S(1)}, bf16[32,1152]{1,0:T(8,128)(2,1)S(1)}, u32[]{:S(2)}, u32[]{:S(2)}) collective-permute-start(bf16[32,1152]{1,0:T(8,128)(2,1)S(1)} %unit_texts.1), channel_id=1, source_target_pairs={{0,16},{1,17},{2,18},{3,19},{4,20},{5,21},{6,22},{7,23},{8,24},{9,... | collective-permute-start | bytes 221192 | tf_op jit(solution)/shard_map/ppermute | solution.py:294
  13.8 4.4 %collective-permute-done.5 = bf16[32,1152]{1,0:T(8,128)(2,1)S(1)} collective-permute-done((bf16[32,1152]{1,0:T(8,128)(2,1)S(1)}, bf16[32,1152]{1,0:T(8,128)(2,1)S(1)}, u32[]{:S(2)}, u32[]{:S(2)}) %collective-permute-start.5) | collective-permute-done | bytes 73760 | tf_op jit(solution)/shard_map/ppermute | solution.py:294
  18.2 1.0 %collective-permute-done.4 = bf16[32,1152]{1,0:T(8,128)(2,1)S(1)} collective-permute-done((bf16[32,1152]{1,0:T(8,128)(2,1)S(1)}, bf16[32,1152]{1,0:T(8,128)(2,1)S(1)}, u32[]{:S(2)}, u32[]{:S(2)}) %collective-permute-start.4) | collective-permute-done | bytes 73760 | tf_op jit(solution)/shard_map/ppermute | solution.py:294
  19.3 1.6 %collective-permute-start.7 = (bf16[128,1152]{1,0:T(8,128)(2,1)S(1)}, bf16[128,1152]{1,0:T(8,128)(2,1)S(1)}, u32[]{:S(2)}, u32[]{:S(2)}) collective-permute-start(bf16[128,1152]{1,0:T(8,128)(2,1)S(1)} %pad_maximum_fusion.texts_a_ref), channel_id=1, source_target_pairs={{0,4},{1,5},{2,6},{3,7},{4,0},{5,1},{6,2},{7,3},{8,12},{9,13},{10,... | collective-permute-start | bytes 884744 | tf_op jit(solution)/shard_map/ppermute | solution.py:294
  21.0 2.2 %collective-permute-start.9 = (bf16[128,384]{1,0:T(8,128)(2,1)S(1)}, bf16[128,384]{1,0:T(8,128)(2,1)S(1)}, u32[]{:S(2)}, u32[]{:S(2)}) collective-permute-start(bf16[128,384]{1,0:T(8,128)(2,1)S(1)} %centre.1), channel_id=1, source_target_pairs={{0,16},{1,17},{2,18},{3,19},{4,20},{5,21},{6,22},{7,23},{8,24},{9,... | collective-permute-start | bytes 294920 | tf_op jit(solution)/shard_map/ppermute | solution.py:294
  23.9 2.4 %collective-permute-done.7.texts_b_ref = bf16[128,1152]{1,0:T(8,128)(2,1)S(1)} collective-permute-done((bf16[128,1152]{1,0:T(8,128)(2,1)S(1)}, bf16[128,1152]{1,0:T(8,128)(2,1)S(1)}, u32[]{:S(2)}, u32[]{:S(2)}) %collective-permute-start.7) | collective-permute-done | bytes 294944 | tf_op jit(solution)/shard_map/ppermute | solution.py:294
  27.0 2.4 %collective-permute-done.9 = bf16[128,384]{1,0:T(8,128)(2,1)S(1)} collective-permute-done((bf16[128,384]{1,0:T(8,128)(2,1)S(1)}, bf16[128,384]{1,0:T(8,128)(2,1)S(1)}, u32[]{:S(2)}, u32[]{:S(2)}) %collective-permute-start.9) | collective-permute-done | bytes 98336 | tf_op jit(solution)/shard_map/ppermute | solution.py:294
  29.5 2.0 %collective-permute-start.12 = (bf16[128,384]{1,0:T(8,128)(2,1)S(1)}, bf16[128,384]{1,0:T(8,128)(2,1)S(1)}, u32[]{:S(2)}, u32[]{:S(2)}) collective-permute-start(bf16[128,384]{1,0:T(8,128)(2,1)S(1)} %centre.1), channel_id=1, source_target_pairs={{0,24},{1,25},{2,26},{3,27},{4,28},{5,29},{6,30},{7,31},{8,16},{9,... | collective-permute-start | bytes 294920 | tf_op jit(solution)/shard_map/ppermute | solution.py:294
  32.1 4.5 %collective-permute-done.12 = bf16[128,384]{1,0:T(8,128)(2,1)S(1)} collective-permute-done((bf16[128,384]{1,0:T(8,128)(2,1)S(1)}, bf16[128,384]{1,0:T(8,128)(2,1)S(1)}, u32[]{:S(2)}, u32[]{:S(2)}) %collective-permute-start.12) | collective-permute-done | bytes 98336 | tf_op jit(solution)/shard_map/ppermute | solution.py:294
  37.5 1.3 %collective-permute-start.15 = (bf16[32,1152]{1,0:T(8,128)(2,1)S(1)}, bf16[32,1152]{1,0:T(8,128)(2,1)S(1)}, u32[]{:S(2)}, u32[]{:S(2)}) collective-permute-start(bf16[32,1152]{1,0:T(8,128)(2,1)S(1)} %grad_project.1), channel_id=1, source_target_pairs={{0,8},{1,9},{2,10},{3,11},{4,12},{5,13},{6,14},{7,15},{8,0},{9,1},... | collective-permute-start | bytes 221192 | tf_op jit(solution)/shard_map/ppermute | solution.py:294
  38.7 1.3 %collective-permute-start.14 = (bf16[32,1152]{1,0:T(8,128)(2,1)S(1)}, bf16[32,1152]{1,0:T(8,128)(2,1)S(1)}, u32[]{:S(2)}, u32[]{:S(2)}) collective-permute-start(bf16[32,1152]{1,0:T(8,128)(2,1)S(1)} %grad_project.1), channel_id=1, source_target_pairs={{0,16},{1,17},{2,18},{3,19},{4,20},{5,21},{6,22},{7,23},{8,24},{9,... | collective-permute-start | bytes 221192 | tf_op jit(solution)/shard_map/ppermute | solution.py:294
  40.1 1.9 %collective-permute-start.13 = (bf16[32,1152]{1,0:T(8,128)(2,1)S(1)}, bf16[32,1152]{1,0:T(8,128)(2,1)S(1)}, u32[]{:S(2)}, u32[]{:S(2)}) collective-permute-start(bf16[32,1152]{1,0:T(8,128)(2,1)S(1)} %grad_project.1), channel_id=1, source_target_pairs={{0,24},{1,25},{2,26},{3,27},{4,28},{5,29},{6,30},{7,31},{8,16},{9,... | collective-permute-start | bytes 221192 | tf_op jit(solution)/shard_map/ppermute | solution.py:294
  42.3 4.6 %collective-permute-done.14 = bf16[32,1152]{1,0:T(8,128)(2,1)S(1)} collective-permute-done((bf16[32,1152]{1,0:T(8,128)(2,1)S(1)}, bf16[32,1152]{1,0:T(8,128)(2,1)S(1)}, u32[]{:S(2)}, u32[]{:S(2)}) %collective-permute-start.14) | collective-permute-done | bytes 73760 | tf_op jit(solution)/shard_map/ppermute | solution.py:294
  48.0 1.1 %collective-permute-start.22 = (bf16[128,1152]{1,0:T(8,128)(2,1)S(1)}, bf16[128,1152]{1,0:T(8,128)(2,1)S(1)}, u32[]{:S(2)}, u32[]{:S(2)}) collective-permute-start(bf16[128,1152]{1,0:T(8,128)(2,1)S(1)} %pad_maximum_fusion.1.own_ref.refs_0_), channel_id=1, source_target_pairs={{0,4},{1,5},{2,6},{3,7},{4,0},{5,1},{6,2},{7,3},{8,12},{9,13},{10,... | collective-permute-start | bytes 884744 | tf_op jit(solution)/shard_map/ppermute | solution.py:294
  49.1 1.9 %collective-permute-start.17 = (bf16[128,1152]{1,0:T(8,128)(2,1)S(1)}, bf16[128,1152]{1,0:T(8,128)(2,1)S(1)}, u32[]{:S(2)}, u32[]{:S(2)}) collective-permute-start(bf16[128,1152]{1,0:T(8,128)(2,1)S(1)} %pad_maximum_fusion.1.own_ref.refs_0_), channel_id=1, source_target_pairs={{0,6},{1,7},{2,4},{3,5},{4,2},{5,3},{6,0},{7,1},{8,14},{9,15},{10,... | collective-permute-start | bytes 884744 | tf_op jit(solution)/shard_map/ppermute | solution.py:294
  51.5 5.5 %collective-permute-done.19.refs_2_.own_ref = bf16[128,1152]{1,0:T(8,128)(2,1)S(1)} collective-permute-done((bf16[128,1152]{1,0:T(8,128)(2,1)S(1)}, bf16[128,1152]{1,0:T(8,128)(2,1)S(1)}, u32[]{:S(2)}, u32[]{:S(2)}) %collective-permute-start.19) | collective-permute-done | bytes 294944 | tf_op jit(solution)/shard_map/ppermute | solution.py:294
  56.9 0.9 %collective-permute-done.22.own_ref = bf16[128,1152]{1,0:T(8,128)(2,1)S(1)} collective-permute-done((bf16[128,1152]{1,0:T(8,128)(2,1)S(1)}, bf16[128,1152]{1,0:T(8,128)(2,1)S(1)}, u32[]{:S(2)}, u32[]{:S(2)}) %collective-permute-start.22) | collective-permute-done | bytes 294944 | tf_op jit(solution)/shard_map/ppermute | solution.py:294
  57.9 6.6 %collective-permute-done.17.own_ref = bf16[128,1152]{1,0:T(8,128)(2,1)S(1)} collective-permute-done((bf16[128,1152]{1,0:T(8,128)(2,1)S(1)}, bf16[128,1152]{1,0:T(8,128)(2,1)S(1)}, u32[]{:S(2)}, u32[]{:S(2)}) %collective-permute-start.17) | collective-permute-done | bytes 294944 | tf_op jit(solution)/shard_map/ppermute | solution.py:294
  64.4 1.1 %grad_features.1 = bf16[128,384]{1,0:T(8,128)(2,1)} custom-call(s32[1]{0:T(128)} %bitcast.place_ref, bf16[384,1152]{1,0:T(8,128)(2,1)S(1)} %copy-done.1, f32[1,1152]{1,0:T(1,128)S(1)} %get-tuple-element.64.weight_sum_ref, bf16[128,1152]{1,0:T(8,128)(2,1)S(1)} %pad_maximum_fusion.1.own_ref.refs_0_, ...), custom_call_target="tpu_custom_call" | custom-call | tf_op jit(solution)/shard_map/grad_features/pallas_call | solution.py:397
  67.1 1.7 %weight.7 = f32[384,1152]{1,0:T(8,128)} custom-call(s32[1]{0:T(128)} %bitcast.place_ref, bf16[512,384]{1,0:T(8,128)(2,1)S(1)} %collective-permute-done.16.normed_ref, bf16[128,1152]{1,0:T(8,128)(2,1)S(1)} %collective-permute-done.17.own_ref, bf16[128,1152]{1,0:T(8,128)(2,1)S(1)} %collective-permute-done.21.other_ref, f32[384,1152]{1,0:T(8,128)S(1)} %weight.6.refs_0_), custom_call_target="tpu_custom_call" | custom-call | flops 226492416 | tf_op jit(solution)/shard_map/weight/pallas_call | solution.py:377
  (54 shorter events, 10.4 us)
Async XLA Ops:
  3.1 1.5 %collective-permute-start = (bf16[64,1280]{1,0:T(8,128)(2,1)S(1)}, bf16[64,1280]{1,0:T(8,128)(2,1)S(1)}, u32[]{:S(2)}, u32[]{:S(2)}) collective-permute-start(bf16[64,1280]{1,0:T(8,128)(2,1)S(1)} %get-tuple-element.37), channel_id=1, source_target_pairs={{0,1},{1,0},{2,3},{3,2},{4,5},{5,4},{6,7},{7,6},{8,9},{9,8},{10,11... | collective-permute-start | bytes 491528 | tf_op jit(solution)/shard_map/ppermute | solution.py:294
  4.8 8.4 %collective-permute-start.1 = (bf16[32,1280]{1,0:T(8,128)(2,1)S(1)}, bf16[32,1280]{1,0:T(8,128)(2,1)S(1)}, u32[]{:S(2)}, u32[]{:S(2)}) collective-permute-start(bf16[32,1280]{1,0:T(8,128)(2,1)S(1)} %get-tuple-element.41), channel_id=1, source_target_pairs={{0,2},{1,3},{2,0},{3,1},{4,6},{5,7},{6,4},{7,5},{8,10},{9,11},{10,... | collective-permute-start | bytes 245768 | tf_op jit(solution)/shard_map/ppermute | solution.py:294
  8.8 5.0 %collective-permute-start.6 = (bf16[32,1152]{1,0:T(8,128)(2,1)S(1)}, bf16[32,1152]{1,0:T(8,128)(2,1)S(1)}, u32[]{:S(2)}, u32[]{:S(2)}) collective-permute-start(bf16[32,1152]{1,0:T(8,128)(2,1)S(1)} %unit_texts.1), channel_id=1, source_target_pairs={{0,8},{1,9},{2,10},{3,11},{4,12},{5,13},{6,14},{7,15},{8,0},{9,1},... | collective-permute-start | bytes 221192 | tf_op jit(solution)/shard_map/ppermute | solution.py:294
  10.4 7.8 %collective-permute-start.5 = (bf16[32,1152]{1,0:T(8,128)(2,1)S(1)}, bf16[32,1152]{1,0:T(8,128)(2,1)S(1)}, u32[]{:S(2)}, u32[]{:S(2)}) collective-permute-start(bf16[32,1152]{1,0:T(8,128)(2,1)S(1)} %unit_texts.1), channel_id=1, source_target_pairs={{0,16},{1,17},{2,18},{3,19},{4,20},{5,21},{6,22},{7,23},{8,24},{9,... | collective-permute-start | bytes 221192 | tf_op jit(solution)/shard_map/ppermute | solution.py:294
  13.0 6.3 %collective-permute-start.4 = (bf16[32,1152]{1,0:T(8,128)(2,1)S(1)}, bf16[32,1152]{1,0:T(8,128)(2,1)S(1)}, u32[]{:S(2)}, u32[]{:S(2)}) collective-permute-start(bf16[32,1152]{1,0:T(8,128)(2,1)S(1)} %unit_texts.1), channel_id=1, source_target_pairs={{0,24},{1,25},{2,26},{3,27},{4,28},{5,29},{6,30},{7,31},{8,16},{9,... | collective-permute-start | bytes 221192 | tf_op jit(solution)/shard_map/ppermute | solution.py:294
  13.4 7.5 %collective-permute-start.2 = (bf16[32,1152]{1,0:T(8,128)(2,1)S(1)}, bf16[32,1152]{1,0:T(8,128)(2,1)S(1)}, u32[]{:S(2)}, u32[]{:S(2)}) collective-permute-start(bf16[32,1152]{1,0:T(8,128)(2,1)S(1)} %get-tuple-element.46), channel_id=1, source_target_pairs={{0,2},{1,3},{2,0},{3,1},{4,6},{5,7},{6,4},{7,5},{8,10},{9,11},{10,... | collective-permute-start | bytes 221192 | tf_op jit(solution)/shard_map/ppermute | solution.py:294
  19.3 7.0 %collective-permute-start.7 = (bf16[128,1152]{1,0:T(8,128)(2,1)S(1)}, bf16[128,1152]{1,0:T(8,128)(2,1)S(1)}, u32[]{:S(2)}, u32[]{:S(2)}) collective-permute-start(bf16[128,1152]{1,0:T(8,128)(2,1)S(1)} %pad_maximum_fusion.texts_a_ref), channel_id=1, source_target_pairs={{0,4},{1,5},{2,6},{3,7},{4,0},{5,1},{6,2},{7,3},{8,12},{9,13},{10,... | collective-permute-start | bytes 884744 | tf_op jit(solution)/shard_map/ppermute | solution.py:294
  21.0 5.3 %collective-permute-start.3 = (bf16[64,1152]{1,0:T(8,128)(2,1)S(1)}, bf16[64,1152]{1,0:T(8,128)(2,1)S(1)}, u32[]{:S(2)}, u32[]{:S(2)}) collective-permute-start(bf16[64,1152]{1,0:T(8,128)(2,1)S(1)} %pad_maximum_fusion.2.images_a_ref), channel_id=1, source_target_pairs={{0,1},{1,0},{2,3},{3,2},{4,5},{5,4},{6,7},{7,6},{8,9},{9,8},{10,11... | collective-permute-start | bytes 442376 | tf_op jit(solution)/shard_map/ppermute | solution.py:294
  21.0 8.3 %collective-permute-start.9 = (bf16[128,384]{1,0:T(8,128)(2,1)S(1)}, bf16[128,384]{1,0:T(8,128)(2,1)S(1)}, u32[]{:S(2)}, u32[]{:S(2)}) collective-permute-start(bf16[128,384]{1,0:T(8,128)(2,1)S(1)} %centre.1), channel_id=1, source_target_pairs={{0,16},{1,17},{2,18},{3,19},{4,20},{5,21},{6,22},{7,23},{8,24},{9,... | collective-permute-start | bytes 294920 | tf_op jit(solution)/shard_map/ppermute | solution.py:294
  23.2 6.3 %collective-permute-start.8 = (bf16[128,384]{1,0:T(8,128)(2,1)S(1)}, bf16[128,384]{1,0:T(8,128)(2,1)S(1)}, u32[]{:S(2)}, u32[]{:S(2)}) collective-permute-start(bf16[128,384]{1,0:T(8,128)(2,1)S(1)} %centre.1), channel_id=1, source_target_pairs={{0,8},{1,9},{2,10},{3,11},{4,12},{5,13},{6,14},{7,15},{8,0},{9,1},... | collective-permute-start | bytes 294920 | tf_op jit(solution)/shard_map/ppermute | solution.py:294
  29.5 2.0 %collective-permute-start.10 = (bf16[64,1152]{1,0:T(8,128)(2,1)S(1)}, bf16[64,1152]{1,0:T(8,128)(2,1)S(1)}, u32[]{:S(2)}, u32[]{:S(2)}) collective-permute-start(bf16[64,1152]{1,0:T(8,128)(2,1)S(1)} %get-tuple-element.52), channel_id=1, source_target_pairs={{0,1},{1,0},{2,3},{3,2},{4,5},{5,4},{6,7},{7,6},{8,9},{9,8},{10,11... | collective-permute-start | bytes 442376 | tf_op jit(solution)/shard_map/ppermute | solution.py:294
  29.5 7.1 %collective-permute-start.12 = (bf16[128,384]{1,0:T(8,128)(2,1)S(1)}, bf16[128,384]{1,0:T(8,128)(2,1)S(1)}, u32[]{:S(2)}, u32[]{:S(2)}) collective-permute-start(bf16[128,384]{1,0:T(8,128)(2,1)S(1)} %centre.1), channel_id=1, source_target_pairs={{0,24},{1,25},{2,26},{3,27},{4,28},{5,29},{6,30},{7,31},{8,16},{9,... | collective-permute-start | bytes 294920 | tf_op jit(solution)/shard_map/ppermute | solution.py:294
  31.5 5.1 %collective-permute-start.11 = (bf16[32,1152]{1,0:T(8,128)(2,1)S(1)}, bf16[32,1152]{1,0:T(8,128)(2,1)S(1)}, u32[]{:S(2)}, u32[]{:S(2)}) collective-permute-start(bf16[32,1152]{1,0:T(8,128)(2,1)S(1)} %get-tuple-element.54), channel_id=1, source_target_pairs={{0,2},{1,3},{2,0},{3,1},{4,6},{5,7},{6,4},{7,5},{8,10},{9,11},{10,... | collective-permute-start | bytes 221192 | tf_op jit(solution)/shard_map/ppermute | solution.py:294
  36.8 10.8 %collective-permute-start.16 = (bf16[512,384]{1,0:T(8,128)(2,1)S(1)}, bf16[512,384]{1,0:T(8,128)(2,1)S(1)}, u32[]{:S(2)}, u32[]{:S(2)}) collective-permute-start(bf16[512,384]{1,0:T(8,128)(2,1)S(1)} %constant_dynamic-update-slice_fusion.normed_ref), channel_id=1, source_target_pairs={{0,4},{1,5},{2,6},{3,7},{4,0},{5,1},{6,2},{7,3},{8,12},{9,13},{10,... | collective-permute-start | bytes 1179656 | tf_op jit(solution)/shard_map/ppermute | solution.py:294
  37.5 4.8 %collective-permute-start.15 = (bf16[32,1152]{1,0:T(8,128)(2,1)S(1)}, bf16[32,1152]{1,0:T(8,128)(2,1)S(1)}, u32[]{:S(2)}, u32[]{:S(2)}) collective-permute-start(bf16[32,1152]{1,0:T(8,128)(2,1)S(1)} %grad_project.1), channel_id=1, source_target_pairs={{0,8},{1,9},{2,10},{3,11},{4,12},{5,13},{6,14},{7,15},{8,0},{9,1},... | collective-permute-start | bytes 221192 | tf_op jit(solution)/shard_map/ppermute | solution.py:294
  38.7 8.2 %collective-permute-start.14 = (bf16[32,1152]{1,0:T(8,128)(2,1)S(1)}, bf16[32,1152]{1,0:T(8,128)(2,1)S(1)}, u32[]{:S(2)}, u32[]{:S(2)}) collective-permute-start(bf16[32,1152]{1,0:T(8,128)(2,1)S(1)} %grad_project.1), channel_id=1, source_target_pairs={{0,16},{1,17},{2,18},{3,19},{4,20},{5,21},{6,22},{7,23},{8,24},{9,... | collective-permute-start | bytes 221192 | tf_op jit(solution)/shard_map/ppermute | solution.py:294
  40.1 6.9 %collective-permute-start.13 = (bf16[32,1152]{1,0:T(8,128)(2,1)S(1)}, bf16[32,1152]{1,0:T(8,128)(2,1)S(1)}, u32[]{:S(2)}, u32[]{:S(2)}) collective-permute-start(bf16[32,1152]{1,0:T(8,128)(2,1)S(1)} %grad_project.1), channel_id=1, source_target_pairs={{0,24},{1,25},{2,26},{3,27},{4,28},{5,29},{6,30},{7,31},{8,16},{9,... | collective-permute-start | bytes 221192 | tf_op jit(solution)/shard_map/ppermute | solution.py:294
  47.5 3.5 %collective-permute-start.18 = (bf16[128,1152]{1,0:T(8,128)(2,1)S(1)}, bf16[128,1152]{1,0:T(8,128)(2,1)S(1)}, u32[]{:S(2)}, u32[]{:S(2)}) collective-permute-start(bf16[128,1152]{1,0:T(8,128)(2,1)S(1)} %pad_maximum_fusion.1.own_ref.refs_0_), channel_id=1, source_target_pairs={{0,1},{1,0},{2,3},{3,2},{4,5},{5,4},{6,7},{7,6},{8,9},{9,8},{10,11... | collective-permute-start | bytes 884744 | tf_op jit(solution)/shard_map/ppermute | solution.py:294
  47.5 9.4 %collective-permute-start.19 = (bf16[128,1152]{1,0:T(8,128)(2,1)S(1)}, bf16[128,1152]{1,0:T(8,128)(2,1)S(1)}, u32[]{:S(2)}, u32[]{:S(2)}) collective-permute-start(bf16[128,1152]{1,0:T(8,128)(2,1)S(1)} %pad_maximum_fusion.1.own_ref.refs_0_), channel_id=1, source_target_pairs={{0,2},{1,3},{2,0},{3,1},{4,6},{5,7},{6,4},{7,5},{8,10},{9,11},{10,... | collective-permute-start | bytes 884744 | tf_op jit(solution)/shard_map/ppermute | solution.py:294
  48.0 9.8 %collective-permute-start.22 = (bf16[128,1152]{1,0:T(8,128)(2,1)S(1)}, bf16[128,1152]{1,0:T(8,128)(2,1)S(1)}, u32[]{:S(2)}, u32[]{:S(2)}) collective-permute-start(bf16[128,1152]{1,0:T(8,128)(2,1)S(1)} %pad_maximum_fusion.1.own_ref.refs_0_), channel_id=1, source_target_pairs={{0,4},{1,5},{2,6},{3,7},{4,0},{5,1},{6,2},{7,3},{8,12},{9,13},{10,... | collective-permute-start | bytes 884744 | tf_op jit(solution)/shard_map/ppermute | solution.py:294
  49.1 15.3 %collective-permute-start.17 = (bf16[128,1152]{1,0:T(8,128)(2,1)S(1)}, bf16[128,1152]{1,0:T(8,128)(2,1)S(1)}, u32[]{:S(2)}, u32[]{:S(2)}) collective-permute-start(bf16[128,1152]{1,0:T(8,128)(2,1)S(1)} %pad_maximum_fusion.1.own_ref.refs_0_), channel_id=1, source_target_pairs={{0,6},{1,7},{2,4},{3,5},{4,2},{5,3},{6,0},{7,1},{8,14},{9,15},{10,... | collective-permute-start | bytes 884744 | tf_op jit(solution)/shard_map/ppermute | solution.py:294
  56.9 7.5 %collective-permute-start.20 = (bf16[128,1152]{1,0:T(8,128)(2,1)S(1)}, bf16[128,1152]{1,0:T(8,128)(2,1)S(1)}, u32[]{:S(2)}, u32[]{:S(2)}) collective-permute-start(bf16[128,1152]{1,0:T(8,128)(2,1)S(1)} %collective-permute-done.19.refs_2_.own_ref), channel_id=1, source_target_pairs={{0,1},{1,0},{2,3},{3,2},{4,5},{5,4},{6,7},{7,6},{8,9},{9,8},{10,11... | collective-permute-start | bytes 884744 | tf_op jit(solution)/shard_map/ppermute | solution.py:294
  57.9 8.2 %collective-permute-start.23 = (bf16[128,1152]{1,0:T(8,128)(2,1)S(1)}, bf16[128,1152]{1,0:T(8,128)(2,1)S(1)}, u32[]{:S(2)}, u32[]{:S(2)}) collective-permute-start(bf16[128,1152]{1,0:T(8,128)(2,1)S(1)} %collective-permute-done.22.own_ref), channel_id=1, source_target_pairs={{0,1},{1,0},{2,3},{3,2},{4,5},{5,4},{6,7},{7,6},{8,9},{9,8},{10,11... | collective-permute-start | bytes 884744 | tf_op jit(solution)/shard_map/ppermute | solution.py:294
  65.5 1.6 %collective-permute-start.21 = (bf16[128,1152]{1,0:T(8,128)(2,1)S(1)}, bf16[128,1152]{1,0:T(8,128)(2,1)S(1)}, u32[]{:S(2)}, u32[]{:S(2)}) collective-permute-start(bf16[128,1152]{1,0:T(8,128)(2,1)S(1)} %collective-permute-done.17.own_ref), channel_id=1, source_target_pairs={{0,1},{1,0},{2,3},{3,2},{4,5},{5,4},{6,7},{7,6},{8,9},{9,8},{10,11... | collective-permute-start | bytes 884744 | tf_op jit(solution)/shard_map/ppermute | solution.py:294
  (5 other events, 48.0 us)
